TPU v7x, 256 devices: a whole 4x4x8 slice. The times are simulated.
256 devices in a mesh: aux: 32 (over y, x, core), occ: 8 (over z).
Axes of the slice: x: 4, y: 4, z: 8, core: 2. Of those that a mesh axis runs over, the one named last changes fastest.
Arguments:
- integrals: bfloat16 [1024, 8, 128, 128], P('aux'), may hold values from -0.008361816 to 0.008361816
- screened_blocks: int32 [1024, 3], P('aux'), may hold values from 0 to 31, as said below
- coeff: bfloat16 [128, 24, 128], P('occ'), may hold values from -6 to 6
- support: int32 [8, 24], replicated, may hold values from 0 to 31, as said below
- metric: bfloat16 [4096, 4096], P('aux'), as said below
- block_order: int32 [32], replicated, may hold values from 0 to 31, each once
Outputs:
- exchange_panel: float32 [32, 128, 128], P('aux')
Inputs may be any that keep to these rules, and one draw needn't show every extreme that they name: `screened_blocks`: column 0 and 1 are shell blocks below 32, column 2 an auxiliary block below 16. Among the 32 rows of one index of aux no mu block appears more than 2 times, and one mu block, the same for all indices, appears exactly 2 times in each. `support`: each row holds 24 different shell blocks. `metric`: Symmetric.
All inputs are finite; a program needn't handle non-finite values.
Results may differ from a plain program's by a relative error of at most 0.00087.
Values may be sent and summed in bfloat16 or wider, within the bound.
A program may use at most 128 MiB of HBM per device.

v0:
```python
import jax
import jax.numpy as jnp
from jax import lax
from jax.sharding import PartitionSpec as P


def body(integrals, screened_blocks, coeff, support, metric, block_order):
    num_triples = integrals.shape[0]
    aux_block = integrals.shape[1]
    shell_size = integrals.shape[2]
    orbitals = coeff.shape[0]
    aux_local = metric.shape[0]
    q_blocks = aux_local // aux_block
    num_owners = lax.axis_size("aux")
    panel_size = orbitals * lax.axis_size("occ")
    mu_list = screened_blocks[:, 0]
    nu_list = screened_blocks[:, 1]
    q_list = screened_blocks[:, 2]
    own_support = lax.dynamic_index_in_dim(support, lax.axis_index("occ"), 0, keepdims=False)
    pick_nu = (own_support[None, :] == nu_list[:, None]).astype(jnp.bfloat16)
    coeff_nu = jnp.einsum("ts,isn->tin", pick_nu, coeff, preferred_element_type=jnp.float32).astype(
        jnp.bfloat16
    )
    half_blocks = jnp.einsum(
        "tamn,tin->taim", integrals, coeff_nu, preferred_element_type=jnp.float32
    ).astype(jnp.bfloat16)
    whole_panel = lax.all_gather(coeff, "occ", axis=0, tiled=True)
    row_support = jnp.repeat(support, orbitals, axis=0)
    pick_mu = (row_support[None, :, :] == mu_list[:, None, None]).astype(jnp.bfloat16)
    coeff_mu = jnp.einsum(
        "tjs,jsm->tjm", pick_mu, whole_panel, preferred_element_type=jnp.float32
    ).astype(jnp.bfloat16)
    term_parts = jnp.einsum(
        "taim,tjm->taij", half_blocks, coeff_mu, preferred_element_type=jnp.float32
    )
    pick_q = (q_list[:, None] == jnp.arange(q_blocks, dtype=jnp.int32)[None, :]).astype(jnp.float32)
    slab_terms = jnp.einsum("tq,taij->qaij", pick_q, term_parts, precision=lax.Precision.HIGHEST)
    slab_terms = slab_terms.reshape(aux_local, orbitals, panel_size).astype(jnp.bfloat16)
    fitted = jnp.einsum(
        "pq,qij->pij",
        metric,
        lax.all_gather(slab_terms, "aux", axis=0, tiled=True),
        preferred_element_type=jnp.float32,
    )
    fitted = fitted.astype(jnp.bfloat16).reshape(q_blocks, aux_block, orbitals, panel_size)
    fitted_rows = fitted[q_list]
    slot_range = jnp.arange(block_order.shape[0], dtype=jnp.int32)
    slot_match = (block_order[None, :] == mu_list[:, None]).astype(jnp.int32)
    slot_index = jnp.sum(slot_match * slot_range[None, :], axis=1)
    capacity = max(2, 2 * num_triples // num_owners)
    triple_range = jnp.arange(num_triples, dtype=jnp.int32)
    earlier = (slot_index[:, None] == slot_index[None, :]) & (
        triple_range[:, None] > triple_range[None, :]
    )
    slot_rank = jnp.sum(earlier.astype(jnp.int32), axis=1)
    owner_range = jnp.arange(num_owners, dtype=jnp.int32)
    cap_range = jnp.arange(capacity, dtype=jnp.int32)
    placing = (slot_index[:, None, None] == owner_range[None, :, None]) & (
        slot_rank[:, None, None] == cap_range[None, None, :]
    )
    placing = placing.astype(jnp.bfloat16)
    send_half = jnp.einsum(
        "tdc,taim->dcaim", placing, half_blocks, preferred_element_type=jnp.float32
    ).astype(jnp.bfloat16)
    send_fit = jnp.einsum(
        "tdc,taij->dcaij", placing, fitted_rows, preferred_element_type=jnp.float32
    ).astype(jnp.bfloat16)
    got_half, got_fit = (
        lax.all_to_all(send_half, "aux", split_axis=0, concat_axis=0, tiled=True),
        lax.all_to_all(send_fit, "aux", split_axis=0, concat_axis=0, tiled=True),
    )
    row_block = lax.dot_general(
        got_half.reshape(-1, shell_size),
        got_fit.reshape(-1, panel_size),
        (((0,), (0,)), ((), ())),
        preferred_element_type=jnp.float32,
    )
    combined = lax.psum(row_block, "occ")
    return combined[None]


def solution(mesh):
    in_specs = (
        P("aux", None, None, None),
        P("aux", None),
        P("occ", None, None),
        P(),
        P("aux", None),
        P(),
    )
    out_specs = P("aux", None, None)
    return jax.shard_map(body, mesh=mesh, in_specs=in_specs, out_specs=out_specs, check_vma=False)
```

profile of v0, /device:TPU:2, one launch (start us, length us, event | category | flops | bytes accessed | tf_op | source)
XLA Modules:
  0.0 269.3 jit_solution(17204373072478834890)
XLA Ops:
  6.5 0.0 all-gather.2.cloned.1.call-start
  6.5 0.8 fusion.42
  7.3 30.0 %all_gather.6 = bf16[128,24,128]{2,1,0:T(8,128)(2,1)S(1)} all-gather(bf16[16,24,128]{2,1,0:T(8,128)(2,1)} %param.8), channel_id=1, replica_groups=mesh['aux'=32,'occ'=8] {'occ'}, dimensions={0}, use_global_device_ids=true | all-gather | bytes 884736 | tf_op jit(solution)/shard_map/all_gather | solution.py:27
  37.4 0.7 dynamic-slice_bitcast_fusion
  38.0 1.2 fusion.15
  39.2 0.0 copy-start.1
  39.3 5.7 %fusion.7 = bf16[32,8,16,128]{3,2,1,0:T(8,128)(2,1)S(1)} fusion(bf16[32,8,128,128]{3,2,1,0:T(8,128)(2,1)} %param.6, bf16[32,16,128,1]{2,0,1,3:T(8,128)(2,1)S(1)} %fusion.15), kind=kOutput, calls=%fused_computation.9 | convolution fusion | flops 134742016 | bytes 9568256 | tf_op jit(solution)/shard_map/tamn,tin->taim/dot_general | solution.py:24
  44.9 1.4 fusion.8
  46.4 0.9 fusion.18
  47.3 0.0 copy-start.2
  47.3 2.0 fusion.11
  49.3 0.1 copy.34
  49.5 0.9 copy.35
  50.4 0.0 all-gather.2.cloned.1.call-update
  50.5 0.2 select_reduce_fusion
  50.6 0.1 convert_reduce_fusion
  50.7 0.9 convolution_convert_fusion.1
  51.7 2.1 copy.31
  53.8 7.7 %all-to-all-start = ((bf16[32,2,8,16,128]{4,3,2,1,0:T(8,128)(2,1)}), bf16[32,2,8,16,128]{4,3,2,1,0:T(8,128)(2,1)}, u32[]{:S(2)}, u32[]{:S(2)}) async-start(bf16[32,2,8,16,128]{4,3,2,1,0:T(8,128)(2,1)} %copy.31), calls=%async_computation | async-start | bytes 4194304 | tf_op jit(solution)/shard_map/all_to_all | solution.py:69
  61.5 0.2 all-reduce.2.cloned.1.call-start
  61.7 82.2 %all-gather.2.cloned.1.call-done = bf16[4096,16,128]{2,0,1:T(8,128)(2,1)} async-done(((bf16[128,16,128]{2,0,1:T(8,128)(2,1)}), bf16[4096,16,128]{2,0,1:T(8,128)(2,1)}) %all-gather.2.cloned.1.call-update) | async-done | bytes 16777232 | tf_op jit(solution)/shard_map/all_gather | solution.py:42
  143.9 8.1 %fusion.14 = bf16[16,8,16,128]{3,1,0,2:T(8,128)(2,1)S(1)} fusion(bf16[4096,16,128]{2,0,1:T(8,128)(2,1)} %all-gather.2.cloned.1.call-done, bf16[128,4096]{1,0:T(8,128)(2,1)S(1)} %copy-done), kind=kOutput, calls=%fused_computation.13 | convolution fusion | flops 2147745792 | bytes 18350080 | tf_op jit(solution)/shard_map/pq,qij->pij/dot_general | solution.py:39
  152.0 0.3 copy.36
  152.4 0.7 gather_fusion
  153.1 0.9 convolution_convert_fusion
  154.1 0.8 copy.38
  154.9 0.0 all-to-all-done
  154.9 32.8 %all_to_all.10 = bf16[32,2,8,16,128]{4,3,2,1,0:T(8,128)(2,1)S(1)} all-to-all(bf16[32,2,8,16,128]{4,3,2,1,0:T(8,128)(2,1)S(1)} %copy.38), channel_id=1, replica_groups=mesh['aux'=32,'occ'=8] {'aux'}, dimensions={0} | all-to-all | bytes 4194304 | tf_op jit(solution)/shard_map/all_to_all | solution.py:70
  187.7 3.0 %convolution_bitcast_fusion = f32[1,128,128]{2,1,0:T(8,128)} fusion(bf16[32,2,8,16,128]{4,3,2,1,0:T(8,128)(2,1)} %all-to-all-done, bf16[32,2,8,16,128]{4,3,2,1,0:T(8,128)(2,1)S(1)} %all_to_all.10), kind=kOutput, calls=%fused_computation.16 | convolution fusion | flops 268435456 | bytes 4259840 | tf_op jit(solution)/shard_map/dot_general | solution.py:72
  190.7 0.0 all-reduce.2.cloned.1.call-update
  190.7 70.2 %all-reduce.2.cloned.1.call-done = f32[1,128,128]{2,1,0:T(8,128)} async-done(((f32[1,128,128]{2,1,0:T(8,128)}), f32[1,128,128]{2,1,0:T(8,128)}) %all-reduce.2.cloned.1.call-update) | async-done | bytes 65552 | tf_op jit(solution)/shard_map/psum | solution.py:78
  260.9 1.5 copy.65
  (8 shorter events, 0.1 us)
Async XLA Ops:
  6.5 137.4 %copy-start = (bf16[128,4096]{1,0:T(8,128)(2,1)S(1)}, bf16[128,4096]{1,0:T(8,128)(2,1)}, u32[]{:S(2)}) copy-start(bf16[128,4096]{1,0:T(8,128)(2,1)} %param.10) | copy-start | bytes 3145732
  6.5 137.4 %all-gather.2.cloned.1.call-start = ((), (), s32[]{:S(2)}) async-start(), calls=%async_computation.2 | async-start | bytes 17301504 | tf_op jit(solution)/shard_map/all_gather | solution.py:42
  39.2 5.7 %copy-start.1 = (s32[8,24]{1,0:T(8,128)S(1)}, s32[8,24]{1,0:T(8,128)}, u32[]{:S(2)}) copy-start(s32[8,24]{1,0:T(8,128)} %param.9) | copy-start | bytes 2308
  47.3 3.1 %copy-start.2 = (s32[32]{0:T(128)S(1)}, s32[32]{0:T(128)}, u32[]{:S(2)}) copy-start(s32[32]{0:T(128)} %param.11) | copy-start | bytes 388
  53.8 101.1 %all-to-all-start = ((bf16[32,2,8,16,128]{4,3,2,1,0:T(8,128)(2,1)}), bf16[32,2,8,16,128]{4,3,2,1,0:T(8,128)(2,1)}, u32[]{:S(2)}, u32[]{:S(2)}) async-start(bf16[32,2,8,16,128]{4,3,2,1,0:T(8,128)(2,1)} %copy.31), calls=%async_computation | async-start | bytes 4194304 | tf_op jit(solution)/shard_map/all_to_all | solution.py:69
  61.5 199.5 %all-reduce.2.cloned.1.call-start = ((), (), s32[]{:S(2)}) async-start(), calls=%async_computation.3 | async-start | bytes 131072 | tf_op jit(solution)/shard_map/psum | solution.py:78
Sparse Core Ops, SparseCore 0:
  50.6 93.3 all-gather.1
  190.8 70.0 all-reduce.1
where the time goes:
time: 270 us; the launch traced here: 269 us
  waiting for transfers between devices  152 us (56%)
  blocking collectives  62.8 us (23%)
  matrix products  24.1 us (9%)
  between operations  13.5 us (5%)
  starting transfers between devices  7.9 us (3%)
  local copies, waits for them, and re-layouts  7.29 us (3%)
    all_gather x1, waiting for transfers between devices, body(): lax.all_gather(slab_terms, 'aux', axis=0, tiled=True)  82.2 us
    psum x1, waiting for transfers between devices, body(): combined = lax.psum(row_block, 'occ')  70.2 us
    all_to_all x1, blocking collectives, body(): lax.all_to_all(send_fit, 'aux', split_axis=0, concat_axis=0, tiled=True)  32.8 us
    all_gather x1, blocking collectives, body(): whole_panel = lax.all_gather(coeff, 'occ', axis=0, tiled=True)  30 us
    dot_general x1, matrix products, body(): jnp.einsum('pq,qij->pij', metric, lax.all_gather(slab_terms, 'aux', axis=...  8.11 us
    all_to_all x1, starting transfers between devices, body(): lax.all_to_all(send_half, 'aux', split_axis=0, concat_axis=0, tiled=True)  7.67 us
    dot_general x1, matrix products, body(): jnp.einsum('tamn,tin->taim', integrals, coeff_nu, preferred_element_type=...  5.67 us
  transfers between devices with their start and end apart: 3, of which 2 were waited for; matrix products, arithmetic and copies ran while one was open for 5% of the time, Pallas kernels for 0%

commit v1 on v0

v1 whole, which is shorter than its diff:
```python
import jax
import jax.numpy as jnp
from jax import lax
from jax.experimental import pallas as pl
from jax.experimental.pallas import tpu as pltpu
from jax.sharding import PartitionSpec as P

MESH = pl.DeviceIdType.MESH
F32 = jnp.float32
BF16 = jnp.bfloat16
NY, NX, NC, NZ = 4, 4, 2, 8
NT, AB, SH, ORB, NSUP, NQ = 32, 8, 128, 16, 24, 16
JL = ORB // NC
HALF = NSUP // NC
LOADS = 8
PER_LOAD = NT // LOADS


def tables(screened_blocks, support, block_order):
    mu, nu, q = screened_blocks[:, 0], screened_blocks[:, 1], screened_blocks[:, 2]
    t = jnp.arange(NT, dtype=jnp.int32)
    before = t[None, :] < t[:, None]
    same_q = q[None, :] == q[:, None]
    rank = jnp.sum(((q[None, :] < q[:, None]) | (same_q & before)).astype(jnp.int32), axis=1)
    follows = jnp.max((same_q & before).astype(jnp.int32), axis=1)
    placed = (rank[None, :] == t[:, None]).astype(jnp.int32)
    order = jnp.sum(placed * t[None, :], axis=1)
    keep = jnp.sum(placed * follows[None, :], axis=1)
    nu_sorted = jnp.sum(placed * nu[None, :], axis=1)
    qs = jnp.arange(NQ, dtype=jnp.int32)
    last = jnp.maximum(jnp.sum((q[None, :] <= qs[:, None]).astype(jnp.int32), axis=1) - 1, 0)
    filled = jnp.max((q[None, :] == qs[:, None]).astype(jnp.int32), axis=1)
    second = jnp.max(((mu[None, :] == mu[:, None]) & before).astype(jnp.int32), axis=1)
    here = (block_order[:, None] == mu[None, :]).astype(jnp.int32)
    one, two = here * (1 - second)[None, :], here * second[None, :]
    t0, t1 = jnp.sum(one * t[None, :], axis=1), jnp.sum(two * t[None, :], axis=1)
    v0, v1 = jnp.sum(one, axis=1), jnp.sum(two, axis=1)
    blocks = jnp.arange(32, dtype=jnp.int32)
    entry = jnp.arange(NSUP, dtype=jnp.int32)
    hit = (support[:, None, :] == blocks[None, :, None]).astype(jnp.int32)
    pos = NSUP + jnp.sum(hit * (entry - NSUP)[None, None, :], axis=2)
    parts = [order, keep, nu_sorted, mu, nu, last, filled, q, q, t0, t1, v0, v1, pos.reshape(-1)]
    parts.append(jnp.zeros((1024 - 4 * 128 + 128 - 256,), jnp.int32))
    return jnp.concatenate(parts).reshape(8, 128)


def kernel(
    ints, coeff, metric, tab, out,
    iv, call, cown, c32, bst, bp, bsend, bps, rbuf, am, at, mg0, mg1, fs0, fs1, fr0, fr1,
    fxs, fxr, ft, bfull, gt, gs, gr, gx, gin, zall, tabr, stab,
    int_sem, own_sem, tab_sem, cs_s, cs_r, cf_s, cf_r, ms_s, ms_r, mf_s, mf_r,
    ex_s, ex_r, mg_s, mg_r, fr_s, fr_r, gx_s, gx_r, z_s, z_r,
):
    d = lax.axis_index("aux")
    z = lax.axis_index("occ")
    y, x, c = d // (NX * NC), (d // NC) % NX, d % NC

    def dev(yy, xx, cc, zz):
        return (yy * (NX * NC) + xx * NC + cc, zz)

    sibling = dev(y, x, 1 - c, z)

    def zpeer(k):
        return dev(y, x, c, (z + k) % NZ)

    def xpeer(k):
        return dev(y, (x + k) % NX, c, z)

    def ypeer(k):
        return dev((y + k) % NY, x, c, z)

    def plane(k):
        return (y + k // NX) % NY, (x + k % NX) % NX

    def copy(src, dst, s, r, to):
        return pltpu.make_async_remote_copy(
            src_ref=src, dst_ref=dst, send_sem=s, recv_sem=r, device_id=to, device_id_type=MESH
        )

    def load(i):
        part = pl.ds(i * PER_LOAD, PER_LOAD)
        return pltpu.make_async_copy(ints.at[part], iv.at[part], int_sem.at[i])

    for i in range(LOADS):
        load(i).start()
    own_tab = pltpu.make_async_copy(tab, stab.at[0], tab_sem.at[0])
    own_tab.start()
    for k in range(NY):
        cols = pl.ds(pl.multiple_of((k * NX + x) * 256, 256), 256)
        pltpu.make_async_copy(metric.at[:, cols], am.at[c, x, k], own_sem.at[0]).start()
        cols = pl.ds(pl.multiple_of((y * NX + k) * 256, 256), 256)
        pltpu.make_async_copy(metric.at[:, cols], at.at[c, y, k], own_sem.at[1]).start()

    barrier = pltpu.get_barrier_semaphore()
    partners = [sibling]
    partners += [zpeer(k) for k in range(1, NZ)]
    partners += [dev(*plane(k), c, z) for k in range(1, NX * NY)]
    for who in partners:
        pl.semaphore_signal(barrier, inc=1, device_id=who, device_id_type=MESH)

    for i in range(ORB):
        c32[pl.ds(i, NSUP, stride=ORB), :] = coeff[i].astype(F32)
    cown[:NSUP] = c32[...].astype(BF16).reshape(NSUP, ORB, SH)
    cown[NSUP] = jnp.zeros((ORB, SH), BF16)
    call[z] = cown[...]
    for k in range(NZ):
        call[k, NSUP] = jnp.zeros((ORB, SH), BF16)

    pl.semaphore_wait(barrier, len(partners))

    half = pl.ds(c * HALF, HALF)
    coeff_sends = []
    for k in (4, 3, 5, 2, 6, 1, 7):
        cp = copy(cown.at[half], call.at[z, half], cs_s.at[k - 1], cs_r.at[k - 1], zpeer(k))
        cp.start()
        coeff_sends.append(cp)
    tab_send = copy(tab, tabr, ex_s.at[0], ex_r.at[0], sibling)
    tab_send.start()
    for k in (2, 1, 3):
        for m in range(NY):
            cols = pl.ds(pl.multiple_of((m * NX + (x + k) % NX) * 256, 256), 256)
            copy(metric.at[:, cols], am.at[c, x, m], ms_s.at[0, k - 1], ms_r.at[0, k - 1], xpeer(k)).start()
            cols = pl.ds(pl.multiple_of(((y + k) % NY * NX + m) * 256, 256), 256)
            copy(metric.at[:, cols], at.at[c, y, m], ms_s.at[1, k - 1], ms_r.at[1, k - 1], ypeer(k)).start()

    own_tab.wait()

    def entry(o, b):
        return stab[0, 3 + o // 4, (o % 4) * 32 + b]

    def half_transform(t, st):
        own = cown[entry(z, stab[0, 0, 96 + t])]
        rhs = jnp.concatenate([iv[t, a] for a in range(AB)], axis=1)
        res = jnp.dot(own, rhs, preferred_element_type=F32)
        for a in range(AB):
            bst[st, pl.ds(a, ORB, stride=AB), :] = res[:, a * SH : (a + 1) * SH]
        bp[t] = bst[st].astype(BF16)

    @pl.loop(0, LOADS)
    def _(i):
        load(i).wait()
        for u in range(PER_LOAD):
            half_transform(i * PER_LOAD + u, u)

    rows_c = pl.ds(pl.multiple_of(c * 64, 64), 64)
    rows_n = pl.ds(pl.multiple_of((1 - c) * 64, 64), 64)

    @pl.loop(0, NT, unroll=4)
    def _(k):
        bsend[k] = bp[stab[0, 0, k], rows_n, :]

    b_send = copy(bsend, bps.at[1], ex_s.at[1], ex_r.at[1], sibling)
    b_send.start()

    @pl.loop(0, NT, unroll=4)
    def _(k):
        bps[0, k] = bp[stab[0, 0, k], rows_c, :]

    forwards = []
    for k in (1, 7, 2, 6, 3, 5, 4):
        src = (z + NZ - k) % NZ
        got = call.at[src, half]
        copy(got, got, cs_s.at[k - 1], cs_r.at[k - 1], zpeer(k)).wait_recv()
        cp = copy(got, got, cf_s.at[k - 1], cf_r.at[k - 1], sibling)
        cp.start()
        forwards.append(cp)
    tab_send.wait_recv()
    sib_tab = pltpu.make_async_copy(tabr, stab.at[1], tab_sem.at[1])
    sib_tab.start()
    sib_tab.wait()
    other = pl.ds((1 - c) * HALF, HALF)
    for k in (1, 7, 2, 6, 3, 5, 4):
        src = (z + NZ - k) % NZ
        got = call.at[src, other]
        copy(got, got, cf_s.at[k - 1], cf_r.at[k - 1], sibling).wait_recv()
    b_send.wait_recv()

    def pick(flag, value):
        return jnp.where(jnp.full(value.shape, flag, jnp.int32) == 1, value, 0.0)

    def panel(b):
        return jnp.concatenate([call[o, entry(o, b)] for o in range(NZ)], axis=0)

    nt = (((1,), (1,)), ((), ()))

    for s in range(NC):
        rbuf[s, 0] = jnp.zeros((64, SH), F32)

    @pl.loop(0, NT, unroll=2)
    def _(k):
        for s in range(NC):
            term = lax.dot_general(bps[s, k], panel(stab[s, 0, 64 + k]), nt, preferred_element_type=F32)
            rbuf[s, k + 1] = term + pick(stab[s, 0, 32 + k], rbuf[s, k])

    for s in range(NC):
        base = (c if s == 0 else 1 - c) * 128

        @pl.loop(0, NQ // 2, unroll=2)
        def _(h):
            got = []
            for u in range(2):
                blk = rbuf[s, stab[s, 1, 32 + 2 * h + u] + 1]
                got.append(pick(stab[s, 1, 48 + 2 * h + u], blk).reshape(JL, AB, SH))
            both = jnp.concatenate(got, axis=1).astype(BF16)
            rows = pl.ds(pl.multiple_of(base + h * 16, 16), 16)
            mg0[y, :, rows, :] = both[:4]
            mg1[x, :, rows, :] = both[4:]

    def m_copy(h, k, j):
        me, buf, to = ((y, mg0, ypeer(k)), (x, mg1, xpeer(k)))[h]
        part = buf.at[me, pl.ds(2 * j, 2)]
        return copy(part, part, mg_s.at[h, k - 1, j], mg_r.at[h, k - 1, j], to)

    def m_wait(h, k, j):
        me, buf, to = ((y, mg0, ypeer(k)), (x, mg1, xpeer(k)))[h]
        part = buf.at[(me + 4 - k) % 4, pl.ds(2 * j, 2)]
        copy(part, part, mg_s.at[h, k - 1, j], mg_r.at[h, k - 1, j], to).wait_recv()

    for j in range(2):
        for k in (2, 1, 3):
            for h in range(2):
                m_copy(h, k, j).start()

    pltpu.make_async_copy(am.at[c, x], am.at[c, x], own_sem.at[0]).wait()
    pltpu.make_async_copy(at.at[c, y], at.at[c, y], own_sem.at[1]).wait()
    for k in range(4):
        for h, (buf, me) in enumerate(((am, x), (at, y))):
            part = buf.at[c, (me + 4 - k) % 4]
            if k > 0:
                copy(part, part, ms_s.at[h, k - 1], ms_r.at[h, k - 1], sibling).wait_recv()
            copy(part, part, mf_s.at[h, k], mf_r.at[h, k], sibling).start()

    @pl.loop(0, NT)
    def _(t):
        rows = panel(stab[0, 1, t])
        for a in range(AB):
            blk = lax.dot_general(rows, iv[t, a], nt, preferred_element_type=F32)
            bfull[t, pl.ds(a * SH, SH), :] = blk.astype(BF16)

    for k in range(4):
        for h, (buf, me) in enumerate(((am, x), (at, y))):
            part = buf.at[1 - c, (me + 4 - k) % 4]
            copy(part, part, mf_s.at[h, k], mf_r.at[h, k], sibling).wait_recv()

    def f_copy(h, k, j):
        src, dst, to = ((fs0, fr0, xpeer(k)), (fs1, fr1, ypeer(k)))[h]
        part = pl.ds(2 * j, 2)
        return copy(src.at[k, part], dst.at[k, part], fr_s.at[h, k - 1, j], fr_r.at[h, k - 1, j], to)

    def fit(h, k, j):
        mat, got, dst, me = ((am, mg0, fs0, x), (at, mg1, fs1, y))[h]
        row = (me + k) % 4
        total = None
        for m in range(4):
            lhs = jnp.concatenate([mat[0, row, m], mat[1, row, m]], axis=0)
            rhs = jnp.concatenate([got[m, 2 * j], got[m, 2 * j + 1]], axis=1)
            term = jnp.dot(lhs, rhs, preferred_element_type=F32)
            total = term if total is None else total + term
        total = total.astype(BF16)
        dst[k, 2 * j] = total[:, :SH]
        dst[k, 2 * j + 1] = total[:, SH:]

    for j in range(2):
        for h in range(2):
            for k in (1, 3, 2):
                m_wait(h, k, j)
        for k in (2, 1, 3):
            for h in range(2):
                fit(h, k, j)
                f_copy(h, k, j).start()
        for h in range(2):
            fit(h, 0, j)

    own_rows = pl.ds(pl.multiple_of(c * 128, 128), 128)
    sib_rows = pl.ds(pl.multiple_of((1 - c) * 128, 128), 128)

    def total_of(h, jj, rows):
        src, got = ((fs0, fr0), (fs1, fr1))[h]
        total = src[0, jj, rows, :].astype(F32)
        for k in range(1, 4):
            total = total + got[k, jj, rows, :].astype(F32)
        return total

    fx = copy(fxs, fxr, ex_s.at[2], ex_r.at[2], sibling)
    for j in range(2):
        for h in range(2):
            for k in (1, 3, 2):
                f_copy(h, k, j).wait_recv()
            for u in range(2):
                fxs[4 * h + 2 * j + u] = total_of(h, 2 * j + u, sib_rows).astype(BF16)
    fx.start()
    for h in range(2):
        for jj in range(4):
            ft[pl.ds(4 * h + jj, 128, stride=ORB), :] = total_of(h, jj, own_rows)
    fx.wait_recv()
    for jj in range(JL):
        ft[pl.ds(JL + jj, 128, stride=ORB), :] = fxr[jj].astype(F32)

    ftq = ft.reshape(NQ, AB * ORB, SH)
    low = pl.ds(pl.multiple_of(c * JL, JL), JL)
    high = pl.ds(pl.multiple_of((1 - c) * JL, JL), JL)

    @pl.loop(0, NT, unroll=2)
    def _(t):
        rows = ftq[stab[0, 1, 64 + t]]
        lhs = jnp.concatenate([rows[a * ORB : (a + 1) * ORB] for a in range(AB)], axis=1)
        lhs = lhs.astype(BF16)
        res = jnp.dot(lhs, bfull[t], preferred_element_type=F32)
        gt[t, low, :] = res[:JL]
        gt[t, high, :] = res[JL:]

    for s in range(32):
        a = pick(stab[0, 2, 64 + s], gt[stab[0, 2, s]])
        b = pick(stab[0, 2, 96 + s], gt[stab[0, 2, 32 + s]])
        gs[s % 2, s // 2] = a + b

    g_send = copy(gs.at[1 - c], gr, ex_s.at[3], ex_r.at[3], sibling)
    g_send.start()
    g_send.wait_recv()
    gx[...] = gs[c] + gr[...]
    sends = []
    for k in (10, 6, 14, 9, 11, 5, 7, 13, 15, 2, 8, 1, 3, 4, 12):
        yy, xx = plane(k)
        cp = copy(gx.at[yy * NX + xx], gin.at[k], gx_s.at[k - 1], gx_r.at[k - 1], dev(yy, xx, c, z))
        cp.start()
        sends.append(cp)
    total = gx[y * NX + x]
    for k in (1, 3, 4, 12, 2, 8, 5, 7, 13, 15, 6, 14, 9, 11, 10):
        copy(gx.at[0], gin.at[k], gx_s.at[k - 1], gx_r.at[k - 1], sibling).wait_recv()
        total = total + gin[k]
    zall[z] = total
    for k in (4, 3, 5, 2, 6, 1, 7):
        cp = copy(zall.at[z], zall.at[z], z_s.at[k - 1], z_r.at[k - 1], zpeer(k))
        cp.start()
        sends.append(cp)
    for k in (1, 7, 2, 6, 3, 5, 4):
        got = zall.at[(z + NZ - k) % NZ]
        copy(got, got, z_s.at[k - 1], z_r.at[k - 1], zpeer(k)).wait_recv()
    out[...] = zall[...].reshape(NZ * ORB, SH).T

    for cp in coeff_sends + forwards + [tab_send, b_send, fx, g_send] + sends:
        cp.wait_send()
    for k in range(4):
        for h, (buf, me) in enumerate(((am, x), (at, y))):
            part = buf.at[c, (me + 4 - k) % 4]
            if k > 0:
                copy(part, part, ms_s.at[h, k - 1], ms_r.at[h, k - 1], sibling).wait_send()
            copy(part, part, mf_s.at[h, k], mf_r.at[h, k], sibling).wait_send()
    for j in range(2):
        for k in (2, 1, 3):
            for h in range(2):
                m_copy(h, k, j).wait_send()
                f_copy(h, k, j).wait_send()


def body(integrals, screened_blocks, coeff, support, metric, block_order):
    tab = tables(screened_blocks, support, block_order)
    vm = pltpu.VMEM
    dma = pltpu.SemaphoreType.DMA
    any_spec = pl.BlockSpec(memory_space=pl.ANY)
    vmem_spec = pl.BlockSpec(memory_space=pltpu.VMEM)
    res = pl.pallas_call(
        kernel,
        out_shape=jax.ShapeDtypeStruct((SH, NZ * ORB), F32),
        in_specs=[any_spec, vmem_spec, any_spec, vmem_spec],
        out_specs=vmem_spec,
        scratch_shapes=[
            vm((NT, AB, SH, SH), BF16),
            vm((NZ, NSUP + 1, ORB, SH), BF16),
            vm((NSUP + 1, ORB, SH), BF16),
            vm((NSUP * ORB, SH), F32),
            vm((PER_LOAD, 128, SH), F32),
            vm((NT, 128, SH), BF16),
            vm((NT, 64, SH), BF16),
            vm((NC, NT, 64, SH), BF16),
            vm((NC, NT + 1, 64, SH), F32),
            vm((NC, 4, 4, 128, 256), BF16),
            vm((NC, 4, 4, 128, 256), BF16),
            vm((4, 4, 256, SH), BF16),
            vm((4, 4, 256, SH), BF16),
            vm((4, 4, 256, SH), BF16),
            vm((4, 4, 256, SH), BF16),
            vm((4, 4, 256, SH), BF16),
            vm((4, 4, 256, SH), BF16),
            vm((JL, 128, SH), BF16),
            vm((JL, 128, SH), BF16),
            vm((128 * ORB, SH), F32),
            vm((NT, AB * SH, SH), BF16),
            vm((NT, ORB, SH), F32),
            vm((NC, 16, ORB, SH), F32),
            vm((16, ORB, SH), F32),
            vm((16, ORB, SH), F32),
            vm((16, ORB, SH), F32),
            vm((NZ, ORB, SH), F32),
            vm((8, 128), jnp.int32),
            pltpu.SMEM((2, 8, 128), jnp.int32),
            dma((LOADS,)), dma((2,)), dma((2,)),
            dma((7,)), dma((7,)), dma((7,)), dma((7,)),
            dma((2, 3)), dma((2, 3)), dma((2, 4)), dma((2, 4)),
            dma((4,)), dma((4,)),
            dma((2, 3, 2)), dma((2, 3, 2)), dma((2, 3, 2)), dma((2, 3, 2)),
            dma((15,)), dma((15,)), dma((7,)), dma((7,)),
        ],
        compiler_params=pltpu.CompilerParams(
            collective_id=0, has_side_effects=True, vmem_limit_bytes=56 * 1024 * 1024
        ),
        cost_estimate=pl.CostEstimate(flops=4 * 10**9, bytes_accessed=10 * 10**6, transcendentals=0),
        name="exchange",
    )(integrals, coeff, metric, tab)
    return res[None]


def solution(mesh):
    in_specs = (
        P("aux", None, None, None),
        P("aux", None),
        P("occ", None, None),
        P(),
        P("aux", None),
        P(),
    )
    return jax.shard_map(
        body, mesh=mesh, in_specs=in_specs, out_specs=P("aux", None, None), check_vma=False
    )
```

time: 270 us -> 73.1 us (0.27)
  waiting for transfers between devices: 152 us -> 0 us
  Pallas kernels: 0 us -> 67.4 us
  blocking collectives: 62.8 us -> 0 us
  matrix products: 24.1 us -> 0 us
  between operations: 13.5 us -> 0.04 us
  starting transfers between devices: 7.9 us -> 0 us
  local copies, waits for them, and re-layouts: 7.29 us -> 3.02 us
    all_gather x1 -> x0, waiting for transfers between devices: 82.2 us -> none  [body(): lax.all_gather(slab_terms, 'aux', axis=0, tiled=True)]
    psum x1 -> x0, waiting for transfers between devices: 70.2 us -> none  [body(): combined = lax.psum(row_block, 'occ')]
    pallas_call x0 -> x1, Pallas kernels: none -> 67.4 us  [body(): pl.pallas_call(kernel, out_shape=jax.ShapeDtypeStruct((SH, NZ * ORB), F32...]
    all_to_all x1 -> x0, blocking collectives: 32.8 us -> none  [body(): lax.all_to_all(send_fit, 'aux', split_axis=0, concat_axis=0, tiled=True)]
    all_gather x1 -> x0, blocking collectives: 30 us -> none  [body(): whole_panel = lax.all_gather(coeff, 'occ', axis=0, tiled=True)]
    dot_general x9 -> x0, matrix products: 24.1 us -> none  [the longest x1 8.11 us: body(): jnp.einsum('pq,qij->pij', metric, lax.all_gather(slab_terms, 'aux', axis=...]
    all_to_all x1 -> x0, starting transfers between devices: 7.67 us -> none  [body(): lax.all_to_all(send_half, 'aux', split_axis=0, concat_axis=0, tiled=True)]
    convert_element_type x4 -> x0, local copies, waits for them, and re-layouts: 4 us -> none  [the longest x1 2.12 us: body(): send_half = jnp.einsum('tdc,taim->dcaim', placing, half_blocks, preferred...]
  transfers between devices with their start and end apart: 3 -> 0, of which waited for: 2 -> 0; matrix products, arithmetic and copies ran while one was open for 5% -> 0% of each run, Pallas kernels for 0% -> 0%
where the time goes in v1:
time: 73.1 us; the launch traced here: 72.7 us
  Pallas kernels  67.4 us (92%)
  local copies, waits for them, and re-layouts  3.02 us (4%)
  other arithmetic  2.25 us (3%)
    pallas_call x1, Pallas kernels, body(): pl.pallas_call(kernel, out_shape=jax.ShapeDtypeStruct((SH, NZ * ORB), F32...  67.4 us
    unnamed x1, local copies, waits for them, and re-layouts  1.47 us

profile of v1, /device:TPU:2, one launch (start us, length us, event | category | flops | bytes accessed | tf_op | source)
XLA Modules:
  0.0 72.7 jit_solution(6256017707886977787)
XLA Ops:
  0.0 0.8 %slice_bitcast_fusion = (s32[32]{0:T(128)S(1)}, s32[32]{0:T(128)S(1)}, s32[32]{0:T(128)S(1)}) fusion(s32[32,3]{0,1:T(4,128)} %param.7), kind=kLoop, calls=%fused_computation.26 | loop fusion | bytes 768 | tf_op jit(solution)/shard_map/squeeze | solution.py:20
  0.8 0.2 convert_reduce_fusion
  1.0 0.1 convert_reduce_fusion.3
  1.1 0.2 convert_reduce_fusion.1
  1.3 0.9 %select_reduce_fusion.1 = (s32[32]{0:T(128)S(1)}, s32[32]{0:T(128)S(1)}, s32[32]{0:T(128)S(1)}, s32[32]{0:T(128)S(1)}, s32[32]{0:T(128)S(1)}, /*index=5*/s32[32]{0:T(128)S(1)}, s32[32]{0:T(128)S(1)}) fusion(s32[32]{0:T(128)S(1)} %convert_reduce_fusion, s32[32]{0:T(128)S(1)} %get-tuple-element.18, s32[32]{0:T(128)} %param.11, ...), kind=kLoop, calls=%fused_computation.2 | loop fusion | flops 16160 | bytes 1792 | tf_op jit(solution)/shard_map/reduce_sum | solution.py:37
  2.3 0.8 %select_reduce_fusion = s32[8,32]{1,0:T(8,128)S(1)} fusion(s32[24]{0:T(128)S(1)} %iota_add_fusion, s32[8,24]{1,0:T(8,128)} %param.9), kind=kLoop, calls=%fused_computation | loop fusion | flops 18176 | bytes 1888 | tf_op jit(solution)/shard_map/reduce_sum | solution.py:41
  3.1 0.1 add.18
  3.2 0.7 concatenate.3
  3.8 67.4 %exchange.1 = f32[128,128]{1,0:T(8,128)} custom-call(bf16[32,8,128,128]{3,2,1,0:T(8,128)(2,1)} %ints.1, bf16[16,24,128]{2,1,0:T(8,128)(2,1)} %coeff.1, bf16[128,4096]{1,0:T(8,128)(2,1)} %metric.1, s32[8,128]{1,0:T(8,128)} %bitcast.9), custom_call_target="tpu_custom_call" | custom-call | flops 4000000000 | bytes 10000000 | tf_op jit(solution)/shard_map/exchange/pallas_call | solution.py:362
  71.2 1.5 %copy.8 = f32[1,128,128]{2,1,0:T(8,128)} copy(f32[1,128,128]{2,1,0:T(8,128)} %bitcast.8) | data formatting | bytes 131072
  (5 shorter events, 0.0 us)

commit v2 on v1

v2 whole, which is shorter than its diff:
```python
import jax
import jax.numpy as jnp
from jax import lax
from jax.experimental import pallas as pl
from jax.experimental.pallas import tpu as pltpu
from jax.sharding import PartitionSpec as P

MESH = pl.DeviceIdType.MESH
F32 = jnp.float32
BF16 = jnp.bfloat16
I32 = jnp.int32
NY, NX, NC, NZ = 4, 4, 2, 8
NT, AB, SH, ORB, NSUP, NQ = 32, 8, 128, 16, 24, 16
JL = ORB // NC
PIECE = NSUP // (NX * NC)
LOADS = 8
PER_LOAD = NT // LOADS
ORDER, KEEP, NUS, MU, NU, LAST, FILLED, QQ, T0, T1, V0, V1, POS = 0, 1, 2, 3, 4, 5, 6, 7, 8, 9, 10, 11, 16
BATCHES = ((1, 2), (6, 2), (3, 3))


def fill_tables(sbv, suv, bov, tabv):
    t = lax.broadcasted_iota(I32, (NT, NT), 0)
    lane = lax.broadcasted_iota(I32, (NT, NT), 1)
    mu, nu, q = [jnp.broadcast_to(sbv[:, i : i + 1], (NT, NT)) for i in range(3)]

    def down(mask, value):
        return jnp.sum(jnp.where(mask, value, 0), axis=0, keepdims=True)

    def across(mask):
        return jnp.sum(jnp.where(mask, 1, 0), axis=1, keepdims=True)

    diagonal, before = t == lane, lane < t
    mu_r, nu_r, q_r = [down(diagonal, v) for v in (mu, nu, q)]
    rank = across((q_r < q) | ((q_r == q) & before))
    follows = across((q_r == q) & before)
    second = across((mu_r == mu) & before)
    placed = rank == lane
    here = bov[...] == mu
    one, two = here & (second == 0), here & (second > 0)
    rows = {
        ORDER: down(placed, t),
        KEEP: down(placed & (follows > 0), 1),
        NUS: down(placed, nu),
        MU: mu_r,
        NU: nu_r,
        LAST: jnp.maximum(down(q <= lane, 1) - 1, 0),
        FILLED: jnp.minimum(down(q == lane, 1), 1),
        QQ: q_r,
        T0: jnp.max(jnp.where(one, t, 0), axis=0, keepdims=True),
        T1: jnp.max(jnp.where(two, t, 0), axis=0, keepdims=True),
        V0: down(one, 1),
        V1: down(two, 1),
    }
    for i, v in rows.items():
        tabv[i : i + 1, 0:NT] = v
    block = lax.broadcasted_iota(I32, (NZ, 32), 1)
    pos = jnp.full((NZ, 32), NSUP, I32)
    for s in range(NSUP):
        pos = jnp.where(jnp.broadcast_to(suv[:, s : s + 1], (NZ, 32)) == block, s, pos)
    tabv[POS : POS + NZ, 0:32] = pos


def kernel(
    ints, coeff, metric, sb, support, border, out,
    cin, sbv, suv, bov, tabv, tabr, stab,
    iv, call, cown, c32, bst, bp, bsend, bps, rbuf, am, at, mg0, mg1, fo, fsend, frelay, fplain, fsum,
    fxs, fxr, ft, bfull, gt, gs, gr, gx, gin, zall,
    in_sem, int_sem, tab_sem, zc_s, zc_r, xc_s, xc_r, cc_s, cc_r, ms_s, ms_r, mf_s, mf_r,
    ex_s, ex_r, mg_s, mg_r, mw_s, mw_r, fp_s, fp_r, gx_s, gx_r, z_s, z_r,
):
    d = lax.axis_index("aux")
    z = lax.axis_index("occ")
    y, x, c = d // (NX * NC), (d // NC) % NX, d % NC

    def dev(yy, xx, cc, zz):
        return (yy * (NX * NC) + xx * NC + cc, zz)

    sibling = dev(y, x, 1 - c, z)

    def zpeer(k):
        return dev(y, x, c, (z + k) % NZ)

    def xpeer(k):
        return dev(y, (x + k) % NX, c, z)

    def ypeer(k):
        return dev((y + k) % NY, x, c, z)

    def plane(k):
        return (y + k // NX) % NY, (x + k % NX) % NX

    def copy(src, dst, s, r, to):
        return pltpu.make_async_remote_copy(
            src_ref=src, dst_ref=dst, send_sem=s, recv_sem=r, device_id=to, device_id_type=MESH
        )

    pending = []

    def start(cp):
        cp.start()
        pending.append(cp)
        return cp

    def load(i):
        part = pl.ds(i * PER_LOAD, PER_LOAD)
        return pltpu.make_async_copy(ints.at[part], iv.at[part], int_sem.at[i])

    small = [
        pltpu.make_async_copy(src, dst, in_sem.at[i])
        for i, (src, dst) in enumerate(((coeff, cin), (sb, sbv), (support, suv), (border, bov)))
    ]
    for cp in small:
        cp.start()
    barrier = pltpu.get_barrier_semaphore()
    partners = [zpeer(k) for k in (4, 3, 5, 2, 6, 1, 7)]
    partners += [dev(*plane(k), c, z) for k in range(1, NX * NY)]
    partners += [sibling]
    for who in partners:
        pl.semaphore_signal(barrier, inc=1, device_id=who, device_id_type=MESH)
    for i in range(LOADS):
        load(i).start()

    def metric_cols(k, m):
        return metric.at[:, pl.ds(pl.multiple_of(((y + k) % NY * NX + m) * 256, 256), 256)]

    for m in range(NX):
        pltpu.make_async_copy(metric_cols(0, m), at.at[c, y, m], in_sem.at[4]).start()

    small[0].wait()
    for i in range(ORB):
        c32[pl.ds(i, NSUP, stride=ORB), :] = cin[i].astype(F32)
    cown[:NSUP] = c32[...].astype(BF16).reshape(NSUP, ORB, SH)
    cown[NSUP] = jnp.zeros((ORB, SH), BF16)
    call[0] = cown[...]
    for k in range(1, NZ):
        call[k, NSUP] = jnp.zeros((ORB, SH), BF16)
    tabv[...] = jnp.zeros(tabv.shape, I32)
    for cp in small[1:]:
        cp.wait()

    pl.semaphore_wait(barrier, len(partners))

    def piece(k):
        return pl.ds(PIECE * (NC * ((x + NX - k) % NX) + c), PIECE)

    for k in (4, 3, 5, 2, 6, 1, 7):
        start(copy(cown.at[piece(0)], call.at[NZ - k, piece(0)], zc_s.at[k - 1], zc_r.at[k - 1], zpeer(k)))
    for k in (2, 1, 3):
        for m in range(NX):
            copy(metric_cols(k, m), at.at[c, y, m], ms_s.at[k - 1], ms_r.at[k - 1], ypeer(k)).start()
        pending.append(copy(at.at[c, y], at.at[c, y], ms_s.at[k - 1], ms_r.at[k - 1], ypeer(k)))

    fill_tables(sbv, suv, bov, tabv)
    own_tab = pltpu.make_async_copy(tabv, stab.at[0], tab_sem.at[0])
    own_tab.start()
    tab_send = start(copy(tabv, tabr, ex_s.at[0], ex_r.at[0], sibling))
    own_tab.wait()

    zr = [(z + r) % NZ for r in range(NZ)]

    def entry(r, b):
        return stab[0, POS + zr[r], b]

    def half_transform(t, st):
        own = cown[entry(0, stab[0, MU, t])]
        rhs = jnp.concatenate([iv[t, a] for a in range(AB)], axis=1)
        res = jnp.dot(own, rhs, preferred_element_type=F32)
        for a in range(AB):
            bst[st, pl.ds(a, ORB, stride=AB), :] = res[:, a * SH : (a + 1) * SH]
        bp[t] = bst[st].astype(BF16)

    def half_loads(lo, hi):
        @pl.loop(lo, hi)
        def _(i):
            load(i).wait()
            for u in range(PER_LOAD):
                half_transform(i * PER_LOAD + u, u)

    def zwait(r):
        got = call.at[r, piece(0)]
        copy(got, got, zc_s.at[NZ - r - 1], zc_r.at[NZ - r - 1], sibling).wait_recv()

    def spread(b):
        lo, n = BATCHES[b]
        part = call.at[pl.ds(lo, n), piece(0)]
        for k in (2, 1, 3):
            start(copy(part, part, xc_s.at[k - 1, b], xc_r.at[k - 1, b], xpeer(k)))
        start(copy(part, part, cc_s.at[0, b], cc_r.at[0, b], sibling))

    def relay(k, b):
        lo, n = BATCHES[b]
        part = call.at[pl.ds(lo, n), piece(k)]
        copy(part, part, xc_s.at[k - 1, b], xc_r.at[k - 1, b], sibling).wait_recv()
        start(copy(part, part, cc_s.at[k, b], cc_r.at[k, b], sibling))

    half_loads(0, LOADS // 2)
    zwait(1)
    zwait(2)
    spread(0)
    zwait(7)
    zwait(6)
    spread(1)
    half_loads(LOADS // 2, LOADS)
    for r in (3, 5, 4):
        zwait(r)
    spread(2)

    rows_c = pl.ds(pl.multiple_of(c * 64, 64), 64)
    rows_n = pl.ds(pl.multiple_of((1 - c) * 64, 64), 64)

    @pl.loop(0, NT, unroll=4)
    def _(k):
        bsend[k] = bp[stab[0, ORDER, k], rows_n, :]

    b_send = start(copy(bsend, bps.at[1], ex_s.at[1], ex_r.at[1], sibling))

    @pl.loop(0, NT, unroll=4)
    def _(k):
        bps[0, k] = bp[stab[0, ORDER, k], rows_c, :]

    tab_send.wait_recv()
    sib_tab = pltpu.make_async_copy(tabr, stab.at[1], tab_sem.at[1])
    sib_tab.start()
    sib_tab.wait()
    for b in range(3):
        for k in (1, 3, 2):
            relay(k, b)
    for b in range(3):
        for k in (0, 1, 3, 2):
            lo, n = BATCHES[b]
            part = call.at[pl.ds(lo, n), pl.ds(PIECE * (NC * ((x + NX - k) % NX) + 1 - c), PIECE)]
            copy(part, part, cc_s.at[k, b], cc_r.at[k, b], sibling).wait_recv()

    def pick(flag, value):
        return jnp.where(jnp.full(value.shape, flag, I32) == 1, value, 0.0)

    def panel(b):
        return jnp.concatenate([call[r, entry(r, b)] for r in range(NZ)], axis=0)

    nt = (((1,), (1,)), ((), ()))

    def m_rows(s):
        base = (c if s == 0 else 1 - c) * 128
        return pl.ds(pl.multiple_of(base, 128), 128)

    def m_part(h, me, j, s):
        return (mg0, mg1)[h].at[me, pl.ds(2 * j, 2), m_rows(s)]

    def ring(h):
        return (y, ypeer) if h == 0 else (x, xpeer)

    def m_copy(h, w, j, s):
        me, to = ring(h)
        part = m_part(h, me, j, s)
        return copy(part, part, mg_s.at[h, w, j, s], mg_r.at[h, w, j, s], to(1 if w == 0 else 3))

    def m_wait(h, w, j, s):
        me, to = ring(h)
        part = m_part(h, (me + (3 if w == 0 else 1)) % 4, j, s)
        copy(part, part, mg_s.at[h, w, j, s], mg_r.at[h, w, j, s], sibling).wait_recv()

    def m_forward(h, j, s):
        me, to = ring(h)
        m_wait(h, j, j, s)
        part = m_part(h, (me + (3 if j == 0 else 1)) % 4, j, s)
        start(copy(part, part, mw_s.at[h, j, s], mw_r.at[h, j, s], to(1 if j == 0 else 3)))

    def m_far(h, j, s):
        me, to = ring(h)
        part = m_part(h, (me + 2) % 4, j, s)
        copy(part, part, mw_s.at[h, j, s], mw_r.at[h, j, s], sibling).wait_recv()

    for s in range(NC):
        if s == 1:
            b_send.wait_recv()
        rbuf[s, 0] = jnp.zeros((64, SH), F32)

        @pl.loop(0, NT, unroll=4)
        def _(k):
            term = lax.dot_general(bps[s, k], panel(stab[s, NUS, k]), nt, preferred_element_type=F32)
            rbuf[s, k + 1] = term + pick(stab[s, KEEP, k], rbuf[s, k])

        for h in range(NQ // 2):
            got = []
            for u in range(2):
                blk = rbuf[s, stab[s, LAST, 2 * h + u] + 1]
                got.append(pick(stab[s, FILLED, 2 * h + u], blk).reshape(JL, AB, SH))
            both = jnp.concatenate(got, axis=1).astype(BF16)
            rows = pl.ds(pl.multiple_of((c if s == 0 else 1 - c) * 128 + h * 16, 16), 16)
            mg0[y, :, rows, :] = both[:4]
            mg1[x, :, rows, :] = both[4:]
        for i in range(2):
            for h in range(2):
                start(m_copy(h, 0, i, s))
                start(m_copy(h, 1, 1 - i, s))

    pltpu.make_async_copy(at.at[c, y], at.at[c, y], in_sem.at[4]).wait()
    for k in range(4):
        part = at.at[c, (y + 4 - k) % 4]
        if k > 0:
            copy(part, part, ms_s.at[k - 1], ms_r.at[k - 1], sibling).wait_recv()
        start(copy(part, part, mf_s.at[k], mf_r.at[k], sibling))

    def full_blocks(lo, hi):
        @pl.loop(lo, hi)
        def _(t):
            rhs = iv[t].reshape(AB * SH, SH)
            blk = lax.dot_general(panel(stab[0, NU, t]), rhs, nt, preferred_element_type=F32).astype(BF16)
            for a in range(AB):
                bfull[t, pl.ds(a * SH, SH), :] = blk[:, a * SH : (a + 1) * SH]

    full_blocks(0, 6)
    for j in range(2):
        for h in range(2):
            m_forward(h, j, 0)
    full_blocks(6, 14)
    for j in range(2):
        for h in range(2):
            m_forward(h, j, 1)
    full_blocks(14, NT)
    for k in range(4):
        part = at.at[1 - c, (y + 4 - k) % 4]
        copy(part, part, mf_s.at[k], mf_r.at[k], sibling).wait_recv()

    @pl.loop(0, NY)
    def _(yy):
        for cc in range(NC):
            for xx in range(NX):
                am[yy, cc, pl.ds(xx * 256, 256), :] = at[cc, yy, xx].T

    def fit(h, j):
        got = (mg0, mg1)[h]
        rhs = [jnp.concatenate([got[m, 2 * j], got[m, 2 * j + 1]], axis=1) for m in range(4)]
        rhs = jnp.concatenate(rhs, axis=0)
        if h == 0:
            lhs = jnp.concatenate([am[m, cc] for m in range(4) for cc in range(NC)], axis=1)
        else:
            lhs = jnp.concatenate(
                [
                    jnp.concatenate([at[cc, yy, m] for m in range(4)], axis=1)
                    for yy in range(NY)
                    for cc in range(NC)
                ],
                axis=0,
            )
        res = jnp.dot(lhs, rhs, preferred_element_type=F32)
        for r in range(4):
            fo[h, j, r, 0] = res[r * 256 : (r + 1) * 256, :SH]
            fo[h, j, r, 1] = res[r * 256 : (r + 1) * 256, SH:]

    def f_copy(h, j, kind):
        me, to = ring(1 - h)
        right = (j == 0) == (kind != 1)
        dst = (frelay, fplain, fsum)[kind]
        return copy(
            fsend.at[h, j, kind], dst.at[h, j], fp_s.at[h, j, kind], fp_r.at[h, j, kind], to(1 if right else 3)
        )

    def f_send(h, j, kind):
        me, to = ring(1 - h)
        off = (2, 3 if j == 0 else 1, 1 if j == 0 else 3)[kind]
        part = fo[h, j, (me + off) % 4]
        if kind == 2:
            f_copy(h, j, 0).wait_recv()
            part = part + frelay[h, j].astype(F32)
        fsend[h, j, kind] = part.astype(BF16)
        start(f_copy(h, j, kind))

    for j in range(2):
        for h in range(2):
            for s in range(NC):
                m_wait(h, 1 - j, j, s)
                m_far(h, j, s)
            fit(h, j)
            f_send(h, j, 0)
            f_send(h, j, 1)
    for j in range(2):
        for h in range(2):
            f_send(h, j, 2)

    own_rows = pl.ds(pl.multiple_of(c * 128, 128), 128)
    sib_rows = pl.ds(pl.multiple_of((1 - c) * 128, 128), 128)

    def total_of(h, j, u, rows):
        me, to = ring(1 - h)
        total = fo[h, j, me, u, rows, :] + fplain[h, j, u, rows, :].astype(F32)
        return total + fsum[h, j, u, rows, :].astype(F32)

    def fx(j):
        part = pl.ds(4 * j, 4)
        return copy(fxs.at[part], fxr.at[part], ex_s.at[2 + j], ex_r.at[2 + j], sibling)

    for j in range(2):
        for h in range(2):
            f_copy(h, j, 1).wait_recv()
            f_copy(h, j, 2).wait_recv()
            for u in range(2):
                fxs[4 * j + 2 * h + u] = total_of(h, j, u, sib_rows).astype(BF16)
        start(fx(j))
        for h in range(2):
            for u in range(2):
                ft[pl.ds(4 * h + 2 * j + u, 128, stride=ORB), :] = total_of(h, j, u, own_rows)
    for j in range(2):
        fx(j).wait_recv()
        for h in range(2):
            for u in range(2):
                ft[pl.ds(JL + 4 * h + 2 * j + u, 128, stride=ORB), :] = fxr[4 * j + 2 * h + u].astype(F32)

    ftq = ft.reshape(NQ, AB * ORB, SH)
    low = pl.ds(pl.multiple_of(c * JL, JL), JL)
    high = pl.ds(pl.multiple_of((1 - c) * JL, JL), JL)

    @pl.loop(0, NT, unroll=8)
    def _(t):
        rows = ftq[stab[0, QQ, t]]
        lhs = jnp.concatenate([rows[a * ORB : (a + 1) * ORB] for a in range(AB)], axis=1)
        res = jnp.dot(lhs.astype(BF16), bfull[t], preferred_element_type=F32)
        gt[t, low, :] = res[:JL]
        gt[t, high, :] = res[JL:]

    for s in range(32):
        one = pick(stab[0, V0, s], gt[stab[0, T0, s]])
        two = pick(stab[0, V1, s], gt[stab[0, T1, s]])
        gs[s % 2, s // 2] = one + two

    g_send = start(copy(gs.at[1 - c], gr, ex_s.at[4], ex_r.at[4], sibling))
    g_send.wait_recv()
    gx[...] = gs[c] + gr[...]
    for k in (10, 6, 14, 9, 11, 5, 7, 13, 15, 2, 8, 1, 3, 4, 12):
        yy, xx = plane(k)
        start(copy(gx.at[yy * NX + xx], gin.at[k], gx_s.at[k - 1], gx_r.at[k - 1], dev(yy, xx, c, z)))
    total = gx[y * NX + x]
    for k in (1, 3, 4, 12, 2, 8, 5, 7, 13, 15, 6, 14, 9, 11, 10):
        copy(gx.at[0], gin.at[k], gx_s.at[k - 1], gx_r.at[k - 1], sibling).wait_recv()
        total = total + gin[k]
    zall[z] = total
    for k in (4, 3, 5, 2, 6, 1, 7):
        start(copy(zall.at[z], zall.at[z], z_s.at[k - 1], z_r.at[k - 1], zpeer(k)))
    for k in (1, 7, 2, 6, 3, 5, 4):
        got = zall.at[(z + NZ - k) % NZ]
        copy(got, got, z_s.at[k - 1], z_r.at[k - 1], zpeer(k)).wait_recv()
    out[...] = zall[...].reshape(NZ * ORB, SH).T

    for cp in pending:
        cp.wait_send()


def body(integrals, screened_blocks, coeff, support, metric, block_order):
    vm = pltpu.VMEM
    dma = pltpu.SemaphoreType.DMA
    any_spec = pl.BlockSpec(memory_space=pl.ANY)
    res = pl.pallas_call(
        kernel,
        out_shape=jax.ShapeDtypeStruct((SH, NZ * ORB), F32),
        in_specs=[any_spec] * 6,
        out_specs=pl.BlockSpec(memory_space=pltpu.VMEM),
        scratch_shapes=[
            vm((ORB, NSUP, SH), BF16),
            vm((NT, 3), I32),
            vm((NZ, NSUP), I32),
            vm((1, 32), I32),
            vm((24, 128), I32),
            vm((24, 128), I32),
            pltpu.SMEM((2, 24, 128), I32),
            vm((NT, AB, SH, SH), BF16),
            vm((NZ, NSUP + 1, ORB, SH), BF16),
            vm((NSUP + 1, ORB, SH), BF16),
            vm((NSUP * ORB, SH), F32),
            vm((PER_LOAD, 128, SH), F32),
            vm((NT, 128, SH), BF16),
            vm((NT, 64, SH), BF16),
            vm((NC, NT, 64, SH), BF16),
            vm((NC, NT + 1, 64, SH), F32),
            vm((NY, NC, 1024, SH), BF16),
            vm((NC, 4, 4, 128, 256), BF16),
            vm((4, 4, 256, SH), BF16),
            vm((4, 4, 256, SH), BF16),
            vm((2, 2, 4, 2, 256, SH), F32),
            vm((2, 2, 3, 2, 256, SH), BF16),
            vm((2, 2, 2, 256, SH), BF16),
            vm((2, 2, 2, 256, SH), BF16),
            vm((2, 2, 2, 256, SH), BF16),
            vm((JL, 128, SH), BF16),
            vm((JL, 128, SH), BF16),
            vm((128 * ORB, SH), F32),
            vm((NT, AB * SH, SH), BF16),
            vm((NT, ORB, SH), F32),
            vm((NC, 16, ORB, SH), F32),
            vm((16, ORB, SH), F32),
            vm((16, ORB, SH), F32),
            vm((16, ORB, SH), F32),
            vm((NZ, ORB, SH), F32),
            dma((5,)), dma((LOADS,)), dma((2,)),
            dma((7,)), dma((7,)), dma((3, 3)), dma((3, 3)), dma((4, 3)), dma((4, 3)),
            dma((3,)), dma((3,)), dma((4,)), dma((4,)),
            dma((5,)), dma((5,)),
            dma((2, 2, 2, 2)), dma((2, 2, 2, 2)), dma((2, 2, 2)), dma((2, 2, 2)),
            dma((2, 2, 3)), dma((2, 2, 3)),
            dma((15,)), dma((15,)), dma((7,)), dma((7,)),
        ],
        compiler_params=pltpu.CompilerParams(
            collective_id=0, has_side_effects=True, vmem_limit_bytes=56 * 1024 * 1024
        ),
        cost_estimate=pl.CostEstimate(flops=4 * 10**9, bytes_accessed=10 * 10**6, transcendentals=0),
        name="exchange",
    )(integrals, coeff, metric, screened_blocks, support, block_order.reshape(1, -1))
    return res[None]


def solution(mesh):
    in_specs = (
        P("aux", None, None, None),
        P("aux", None),
        P("occ", None, None),
        P(),
        P("aux", None),
        P(),
    )
    return jax.shard_map(
        body, mesh=mesh, in_specs=in_specs, out_specs=P("aux", None, None), check_vma=False
    )
```

time: 73.1 us -> 66.9 us (0.915)
  Pallas kernels: 67.4 us -> 63.9 us
  other arithmetic: 2.25 us -> 0 us
    pallas_call x1, Pallas kernels: 67.4 us -> 63.9 us  [body(): pl.pallas_call(kernel, out_shape=jax.ShapeDtypeStruct((SH, NZ * ORB), F32...]
    reduce_sum x2 -> x0, other arithmetic: 1.75 us -> none  [the longest x1 0.95 us: tables(): v0, v1 = (jnp.sum(one, axis=1), jnp.sum(two, axis=1))]
    unnamed x1 -> x2, local copies, waits for them, and re-layouts: 1.47 us -> 2.84 us
    squeeze x1 -> x0, local copies, waits for them, and re-layouts: 0.8 us -> none  [tables(): screened_blocks[:, 0]]
where the time goes in v2:
time: 66.9 us; the launch traced here: 66.7 us
  Pallas kernels  63.9 us (96%)
  local copies, waits for them, and re-layouts  2.84 us (4%)
    pallas_call x1, Pallas kernels, body(): pl.pallas_call(kernel, out_shape=jax.ShapeDtypeStruct((SH, NZ * ORB), F32...  63.9 us
    unnamed x2, local copies, waits for them, and re-layouts  2.84 us

profile of v2, /device:TPU:2, one launch (start us, length us, event | category | flops | bytes accessed | tf_op | source)
XLA Modules:
  0.0 66.7 jit_solution(14636241581274039924)
XLA Ops:
  0.0 1.4 %copy.7.sb = s32[32,3]{1,0:T(8,128)} copy(s32[32,3]{0,1:T(4,128)} %param.7) | data formatting | bytes 768 | tf_op args[1]
  1.4 63.9 %exchange.1 = f32[128,128]{1,0:T(8,128)} custom-call(bf16[32,8,128,128]{3,2,1,0:T(8,128)(2,1)} %ints.1, bf16[16,24,128]{2,1,0:T(8,128)(2,1)} %coeff.1, bf16[128,4096]{1,0:T(8,128)(2,1)} %metric.1, s32[32,3]{1,0:T(8,128)} %copy.7.sb, s32[8,24]{1,0:T(8,128)} %support.1, s32[1,32]{1,0:T(1,128)} %bitcast.3), custom_call_target="tpu_custom_call" | custom-call | flops 4000000000 | bytes 10000000 | tf_op jit(solution)/shard_map/exchange/pallas_call | solution.py:453
  65.2 1.5 %copy.9 = f32[1,128,128]{2,1,0:T(8,128)} copy(f32[1,128,128]{2,1,0:T(8,128)} %bitcast.2) | data formatting | bytes 131072

commit v3 on v2

v3 whole, which is shorter than its diff:
```python
import jax
import jax.numpy as jnp
from jax import lax
from jax.experimental import pallas as pl
from jax.experimental.pallas import tpu as pltpu
from jax.sharding import PartitionSpec as P

MESH = pl.DeviceIdType.MESH
F32 = jnp.float32
BF16 = jnp.bfloat16
I32 = jnp.int32
NY, NX, NC, NZ = 4, 4, 2, 8
NT, AB, SH, ORB, NSUP, NQ = 32, 8, 128, 16, 24, 16
JL = ORB // NC
PIECE = NSUP // (NX * NC)
LOADS = 8
PER_LOAD = NT // LOADS
ORDER, KEEP, NUS, MU, NU, LAST, FILLED, QQ, T0, T1, V0, V1, POS = 0, 1, 2, 3, 4, 5, 6, 7, 8, 9, 10, 11, 16
BATCHES = ((0, 1, 2), (0, 3, 1), (1, 0, 4))
GROUPS = ((0, 1, 2, 7), (3, 4, 5, 6))


def fill_tables(sbv, suv, bov, tabv):
    t = lax.broadcasted_iota(I32, (NT, NT), 0)
    lane = lax.broadcasted_iota(I32, (NT, NT), 1)

    def down(mask, value):
        return jnp.sum(jnp.where(mask, value, 0), axis=0, keepdims=True)

    def across(mask, value=1):
        return jnp.sum(jnp.where(mask, value, 0), axis=1, keepdims=True)

    diagonal, before = t == lane, lane < t
    mu_r, nu_r, q_r = [sbv[i : i + 1, :] for i in range(3)]
    mu, nu, q = [across(diagonal, v) for v in (mu_r, nu_r, q_r)]
    rank = across((q_r < q) | ((q_r == q) & before))
    follows = across((q_r == q) & before)
    second = across((mu_r == mu) & before)
    placed = rank == lane
    here = bov[...] == mu
    one, two = here & (second == 0), here & (second > 0)
    rows = {
        ORDER: down(placed, t),
        KEEP: down(placed & (follows > 0), 1),
        NUS: down(placed, jnp.broadcast_to(nu, (NT, NT))),
        MU: mu_r,
        NU: nu_r,
        LAST: jnp.maximum(down(q <= lane, 1) - 1, 0),
        FILLED: jnp.minimum(down(q == lane, 1), 1),
        QQ: q_r,
        T0: jnp.max(jnp.where(one, t, 0), axis=0, keepdims=True),
        T1: jnp.max(jnp.where(two, t, 0), axis=0, keepdims=True),
        V0: down(one, 1),
        V1: down(two, 1),
    }
    for i, v in rows.items():
        tabv[i : i + 1, 0:NT] = v
    block = lax.broadcasted_iota(I32, (NZ, 32), 1)
    pos = jnp.full((NZ, 32), NSUP, I32)
    for s in range(NSUP):
        pos = jnp.where(jnp.broadcast_to(suv[:, s : s + 1], (NZ, 32)) == block, s, pos)
    tabv[POS : POS + NZ, 0:32] = pos


def kernel(
    ints, coeff, metric, sb, support, border, out,
    cin, sbv, suv, bov, tabv, tabr, stab,
    iv, calla, callb, cown, c32, bst, bp, bsend, bps, rbuf, nat, tra, natt, trat, mg0, mg1, fo, fsend, fgot,
    fxs, fxr, ta, ft, bfull, gt, gs, gr, gx, gin, zall,
    in_sem, int_sem, tab_sem, zc_s, zc_r, xc_s, xc_r, cc_s, cc_r, ms_s, ms_r, mf_s, mf_r,
    ex_s, ex_r, mg_s, mg_r, fa_s, fa_r, fx_s, fx_r, gx_s, gx_r, z_s, z_r,
):
    d = lax.axis_index("aux")
    z = lax.axis_index("occ")
    y, x, c = d // (NX * NC), (d // NC) % NX, d % NC
    ys, xs, zs = [[lax.rem(v + k, n) for k in range(n)] for v, n in ((y, NY), (x, NX), (z, NZ))]

    def dev(yy, xx, cc, zz):
        return (yy * (NX * NC) + xx * NC + cc, zz)

    sibling = dev(y, x, 1 - c, z)

    def zpeer(k):
        return dev(y, x, c, zs[k])

    def xpeer(k):
        return dev(y, xs[k], c, z)

    def ypeer(k):
        return dev(ys[k], x, c, z)

    def plane(k):
        return ys[k // NX], xs[k % NX]

    def copy(src, dst, s, r, to):
        return pltpu.make_async_remote_copy(
            src_ref=src, dst_ref=dst, send_sem=s, recv_sem=r, device_id=to, device_id_type=MESH
        )

    pending = []

    def start(cp):
        cp.start()
        pending.append(cp)
        return cp

    def load(i):
        part = pl.ds(i * PER_LOAD, PER_LOAD)
        return pltpu.make_async_copy(ints.at[part], iv.at[part], int_sem.at[i])

    small = [
        pltpu.make_async_copy(src, dst, in_sem.at[i])
        for i, (src, dst) in enumerate(((coeff, cin), (sb, sbv), (support, suv), (border, bov)))
    ]
    for cp in small:
        cp.start()
    barrier = pltpu.get_barrier_semaphore()
    partners = [zpeer(k) for k in (4, 3, 5, 2, 6, 1, 7)]
    partners += [dev(*plane(k), c, z) for k in range(1, NX * NY)]
    partners += [sibling]
    partners += [dev(y, xs[k], 1 - c, z) for k in (1, 2, 3)]
    partners += [dev(ys[k], x, 1 - c, z) for k in (1, 2, 3)]
    for who in partners:
        pl.semaphore_signal(barrier, inc=1, device_id=who, device_id_type=MESH)
    for i in range(LOADS):
        load(i).start()

    def metric_part(h, k, m):
        if h == 0:
            col = (ys[k] * NX + m) * 256 + c * 128
        else:
            col = (m * NX + xs[k]) * 256 + (1 - c) * 128
        return metric.at[:, pl.ds(pl.multiple_of(col, 128), 128)]

    quarters = ((nat, ys, ypeer), (tra, xs, xpeer))
    for h, (buf, me, to) in enumerate(quarters):
        for m in range(4):
            pltpu.make_async_copy(metric_part(h, 0, m), buf.at[c, me[0], m], in_sem.at[4 + h]).start()

    small[0].wait()
    for i in range(ORB):
        c32[pl.ds(i, NSUP, stride=ORB), :] = cin[i].astype(F32)
    cown[:NSUP] = c32[...].astype(BF16).reshape(NSUP, ORB, SH)
    cown[NSUP] = jnp.zeros((ORB, SH), BF16)
    calla[0] = cown[...]
    for k in range(NZ // 2):
        calla[k, NSUP] = jnp.zeros((ORB, SH), BF16)
        callb[k, NSUP] = jnp.zeros((ORB, SH), BF16)
    tabv[...] = jnp.zeros(tabv.shape, I32)
    for cp in small[1:]:
        cp.wait()

    pl.semaphore_wait(barrier, len(partners))

    place = [xs[k] * (1 - c) + ys[k] * c for k in range(4)]
    place_n = [xs[k] * c + ys[k] * (1 - c) for k in range(4)]

    calls = (calla, callb)

    def spot(r):
        g = int(r in GROUPS[1])
        return calls[g].at[GROUPS[g].index(r)]

    def batch(b, part):
        g, lo, n = BATCHES[b]
        return calls[g].at[pl.ds(lo, n), part]

    def piece(k):
        return pl.ds(c * (NSUP // NC) + PIECE * place[(4 - k) % 4], PIECE)

    def piece_n(k):
        return pl.ds((1 - c) * (NSUP // NC) + PIECE * place_n[(4 - k) % 4], PIECE)

    def qpeer(k):
        return dev(ys[k] * c + y * (1 - c), xs[k] * (1 - c) + x * c, c, z)

    for k in (7, 1, 6, 4, 3, 5, 2):
        start(copy(cown.at[piece(0)], spot(NZ - k).at[piece(0)], zc_s.at[k - 1], zc_r.at[k - 1], zpeer(k)))
    for k in (2, 1, 3):
        for h, (buf, me, to) in enumerate(quarters):
            for m in range(4):
                part = buf.at[c, me[0], m]
                copy(metric_part(h, k, m), part, ms_s.at[h, k - 1], ms_r.at[h, k - 1], to(k)).start()
            part = buf.at[c, me[0]]
            pending.append(copy(part, part, ms_s.at[h, k - 1], ms_r.at[h, k - 1], to(k)))

    fill_tables(sbv, suv, bov, tabv)
    own_tab = pltpu.make_async_copy(tabv, stab.at[0], tab_sem.at[0])
    own_tab.start()
    tab_send = start(copy(tabv, tabr, ex_s.at[0], ex_r.at[0], sibling))
    own_tab.wait()

    zr = zs

    def entry(r, b):
        return stab[0, POS + zr[r], b]

    def half_transform(t, st):
        own = cown[entry(0, stab[0, MU, t])]
        rhs = jnp.concatenate([iv[t, a] for a in range(AB)], axis=1)
        res = jnp.dot(own, rhs, preferred_element_type=F32)
        for a in range(AB):
            bst[st, pl.ds(a, ORB, stride=AB), :] = res[:, a * SH : (a + 1) * SH]
        bp[t] = bst[st].astype(BF16)

    def half_loads(lo, hi):
        @pl.loop(lo, hi)
        def _(i):
            load(i).wait()
            for u in range(PER_LOAD):
                half_transform(i * PER_LOAD + u, u)

    def zwait(r):
        got = spot(r).at[piece(0)]
        copy(got, got, zc_s.at[NZ - r - 1], zc_r.at[NZ - r - 1], sibling).wait_recv()

    def spread(b):
        part = batch(b, piece(0))
        for k in (2, 1, 3):
            start(copy(part, part, xc_s.at[k - 1, b], xc_r.at[k - 1, b], qpeer(k)))
        start(copy(part, part, cc_s.at[0, b], cc_r.at[0, b], sibling))

    def relay(k, b):
        part = batch(b, piece(k))
        copy(part, part, xc_s.at[k - 1, b], xc_r.at[k - 1, b], sibling).wait_recv()
        start(copy(part, part, cc_s.at[k, b], cc_r.at[k, b], sibling))

    half_loads(0, LOADS // 2)
    zwait(7)
    spread(1)
    zwait(1)
    zwait(2)
    spread(0)
    half_loads(LOADS // 2, LOADS)

    rows_c = pl.ds(pl.multiple_of(c * 64, 64), 64)
    rows_n = pl.ds(pl.multiple_of((1 - c) * 64, 64), 64)

    @pl.loop(0, NT, unroll=4)
    def _(k):
        bsend[k] = bp[stab[0, ORDER, k], rows_n, :]

    b_send = start(copy(bsend, bps.at[1], ex_s.at[1], ex_r.at[1], sibling))

    @pl.loop(0, NT, unroll=4)
    def _(k):
        bps[0, k] = bp[stab[0, ORDER, k], rows_c, :]

    for r in (6, 3, 5, 4):
        zwait(r)
    spread(2)

    def got_panel(b):
        for k in (0, 1, 3, 2):
            part = batch(b, piece_n(k))
            copy(part, part, cc_s.at[k, b], cc_r.at[k, b], sibling).wait_recv()

    mfs = []
    for h, (buf, me, to) in enumerate(quarters):
        pltpu.make_async_copy(buf.at[c, me[0]], buf.at[c, me[0]], in_sem.at[4 + h]).wait()
        for k in (1, 3, 2):
            part = buf.at[c, me[4 - k]]
            copy(part, part, ms_s.at[h, k - 1], ms_r.at[h, k - 1], sibling).wait_recv()
        mfs.append(start(copy(buf.at[c], buf.at[c], mf_s.at[h], mf_r.at[h], sibling)))

    def transpose_quarters(cc):
        @pl.loop(0, 4)
        def _(i):
            for j in range(4):
                natt[cc, j, i] = nat[cc, i, j].T
                trat[cc, j, i] = tra[cc, i, j].T

    tab_send.wait_recv()
    sib_tab = pltpu.make_async_copy(tabr, stab.at[1], tab_sem.at[1])
    sib_tab.start()
    sib_tab.wait()
    for b in (1, 0):
        for k in (1, 3, 2):
            relay(k, b)
    transpose_quarters(c)
    for b in (1, 0):
        got_panel(b)

    def pick(flag, value):
        return jnp.where(jnp.full(value.shape, flag, I32) == 1, value, 0.0)

    def panel(b, groups):
        return jnp.concatenate([calls[g][i, entry(GROUPS[g][i], b)] for g in groups for i in range(4)], axis=0)

    nt = (((1,), (1,)), ((), ()))

    def m_rows(s):
        base = (c if s == 0 else 1 - c) * 128
        return pl.ds(pl.multiple_of(base, 128), 128)

    def m_part(h, me, j, s):
        return (mg0, mg1)[h].at[me, pl.ds(2 * j, 2), m_rows(s)]

    def ring(h):
        return (ys, ypeer) if h == 0 else (xs, xpeer)

    def m_copy(h, k, j, s):
        me, to = ring(h)
        part = m_part(h, me[0], j, s)
        return copy(part, part, mg_s.at[h, k - 1, j, s], mg_r.at[h, k - 1, j, s], to(k))

    def m_wait(h, j):
        me, to = ring(h)
        for s in range(NC):
            for k in (1, 3, 2):
                part = m_part(h, me[4 - k], j, s)
                copy(part, part, mg_s.at[h, k - 1, j, s], mg_r.at[h, k - 1, j, s], sibling).wait_recv()

    def m_send(j, s):
        for k in (2, 1, 3):
            for h in range(2):
                start(m_copy(h, k, j, s))

    def m_terms(g, s):
        rbuf[s, 0] = jnp.zeros((32, SH), F32)

        @pl.loop(0, NT, unroll=8)
        def _(k):
            part = panel(stab[s, NUS, k], (g,))
            none = jnp.zeros_like(part)
            rhs = [jnp.concatenate([part, none], axis=1), jnp.concatenate([none, part], axis=1)]
            lhs = jnp.concatenate([bps[s, k, :32], bps[s, k, 32:]], axis=1)
            term = lax.dot_general(lhs, jnp.concatenate(rhs, axis=0), nt, preferred_element_type=F32)
            rbuf[s, k + 1] = term + pick(stab[s, KEEP, k], rbuf[s, k])

        for h in range(NQ // 2):
            got = []
            for u in range(2):
                blk = rbuf[s, stab[s, LAST, 2 * h + u] + 1]
                got.append(pick(stab[s, FILLED, 2 * h + u], blk).reshape(4, AB, SH))
            both = jnp.concatenate(got, axis=1).astype(BF16)
            rows = pl.ds(pl.multiple_of((c if s == 0 else 1 - c) * 128 + h * 16, 16), 16)
            mg0[y, 2 * g : 2 * g + 2, rows, :] = both[:2]
            mg1[x, 2 * g : 2 * g + 2, rows, :] = both[2:]
        m_send(g, s)

    m_terms(0, 0)
    for k in (1, 3, 2):
        relay(k, 2)
    b_send.wait_recv()
    m_terms(0, 1)
    got_panel(2)

    def full_blocks(lo, hi):
        @pl.loop(lo, hi)
        def _(t):
            rhs = iv[t].reshape(AB * SH, SH)
            blk = lax.dot_general(panel(stab[0, NU, t], (0, 1)), rhs, nt, preferred_element_type=F32).astype(BF16)
            for a in range(AB):
                bfull[t, pl.ds(a * SH, SH), :] = blk[:, a * SH : (a + 1) * SH]

    def fit(h, j):
        got = (mg0, mg1)[h]
        rhs = [jnp.concatenate([got[m, 2 * j], got[m, 2 * j + 1]], axis=1) for m in range(4)]
        rhs = jnp.concatenate(rhs, axis=0)
        same, cross = ((natt, tra), (nat, trat))[h]
        if h == 0:
            lhs = [
                [(same if cr == ck else cross)[cr, r, k] for k in range(4) for ck in range(NC)]
                for r in range(4)
                for cr in range(NC)
            ]
        else:
            lhs = [
                [(same if cr == ck else cross)[ck, r, k] for k in range(4) for ck in range(NC)]
                for r in range(4)
                for cr in range(NC)
            ]
        lhs = jnp.concatenate([jnp.concatenate(v, axis=1) for v in lhs], axis=0)
        res = jnp.dot(lhs, rhs, preferred_element_type=F32)
        for r in range(4):
            fo[h, j, r, 0] = res[r * 256 : (r + 1) * 256, :SH]
            fo[h, j, r, 1] = res[r * 256 : (r + 1) * 256, SH:]

    def f_part(h, j, off):
        return fo.at[h, j, (xs, ys)[h][off]]

    def f_copy(h, j, k, cc):
        src = fsend.at[h, j, k - 1, :, pl.ds(cc * 128, 128)]
        to = dev(y, xs[k], cc, z) if h == 0 else dev(ys[k], x, cc, z)
        return copy(src, fgot.at[c, k - 1, h, j], fa_s.at[h, j, k - 1, cc], fa_r.at[h, j, k - 1, c], to)

    def fx(h, j):
        return copy(fxs.at[h, j], fxr.at[h, j], fx_s.at[h, j], fx_r.at[h, j], sibling)

    own_rows = pl.ds(pl.multiple_of(c * 128, 128), 128)
    sib_rows = pl.ds(pl.multiple_of((1 - c) * 128, 128), 128)

    def fits(j):
        for h in range(2):
            m_wait(h, j)
            fit(h, j)
            for k in (2, 1, 3):
                fsend[h, j, k - 1] = f_part(h, j, k)[...].astype(BF16)
                for cc in range(NC):
                    start(f_copy(h, j, k, cc))
            fxs[h, j] = f_part(h, j, 0)[:, sib_rows].astype(BF16)
            start(fx(h, j))

    def got_from(cs, h, j, u):
        total = f_part(h, j, 0)[u, own_rows] if cs is c else fxr[h, j, u].astype(F32)
        for k in range(3):
            total = total + fgot[cs, k, h, j, u].astype(F32)
        return total

    def totals(j):
        left = lax.broadcasted_iota(I32, (128, SH), 1) < 64
        for h in range(2):
            fx(h, j).wait_recv()
            for k in (1, 3, 2):
                for cc in range(NC):
                    part = fgot.at[cc, k - 1, h, j]
                    copy(part, part, fa_s.at[h, j, k - 1, cc], fa_r.at[h, j, k - 1, cc], sibling).wait_recv()
            for u in range(2):
                for w, cs in enumerate((c, 1 - c)):
                    val = got_from(cs, h, j, u)
                    if j == 0:
                        ta[w, 2 * h + u] = val
                    else:
                        old = ta[w, 2 * h + u]
                        row = JL * w + 2 * h + u
                        ft[pl.ds(row, 128, stride=ORB), :] = jnp.where(left, old, pltpu.roll(val, 64, axis=1))
                        ft[pl.ds(row + 4, 128, stride=ORB), :] = jnp.where(left, pltpu.roll(old, 64, axis=1), val)

    m_terms(1, 0)
    m_terms(1, 1)
    for cp in mfs:
        cp.wait_recv()
    transpose_quarters(1 - c)
    full_blocks(0, 10)
    fits(0)
    full_blocks(10, 24)
    fits(1)
    full_blocks(24, NT)
    totals(0)
    totals(1)

    ftq = ft.reshape(NQ, AB * ORB, SH)
    low = pl.ds(pl.multiple_of(c * JL, JL), JL)
    high = pl.ds(pl.multiple_of((1 - c) * JL, JL), JL)

    @pl.loop(0, NT, unroll=8)
    def _(t):
        rows = ftq[stab[0, QQ, t]]
        lhs = jnp.concatenate([rows[a * ORB : (a + 1) * ORB] for a in range(AB)], axis=1)
        res = jnp.dot(lhs.astype(BF16), bfull[t], preferred_element_type=F32)
        gt[t, low, :] = res[:JL]
        gt[t, high, :] = res[JL:]

    for s in range(32):
        one = pick(stab[0, V0, s], gt[stab[0, T0, s]])
        two = pick(stab[0, V1, s], gt[stab[0, T1, s]])
        gs[s % 2, s // 2] = one + two

    g_send = start(copy(gs.at[1 - c], gr, ex_s.at[4], ex_r.at[4], sibling))
    g_send.wait_recv()
    gx[...] = gs[c] + gr[...]
    for k in (10, 6, 14, 9, 11, 5, 7, 13, 15, 2, 8, 1, 3, 4, 12):
        yy, xx = plane(k)
        start(copy(gx.at[yy * NX + xx], gin.at[k], gx_s.at[k - 1], gx_r.at[k - 1], dev(yy, xx, c, z)))
    total = gx[y * NX + x]
    for k in (1, 3, 4, 12, 2, 8, 5, 7, 13, 15, 6, 14, 9, 11, 10):
        copy(gx.at[0], gin.at[k], gx_s.at[k - 1], gx_r.at[k - 1], sibling).wait_recv()
        total = total + gin[k]
    zall[z] = total
    for k in (4, 3, 5, 2, 6, 1, 7):
        start(copy(zall.at[z], zall.at[z], z_s.at[k - 1], z_r.at[k - 1], zpeer(k)))
    for k in (1, 7, 2, 6, 3, 5, 4):
        got = zall.at[zs[NZ - k]]
        copy(got, got, z_s.at[k - 1], z_r.at[k - 1], zpeer(k)).wait_recv()
    out[...] = zall[...].reshape(NZ * ORB, SH)

    for cp in pending:
        cp.wait_send()


def body(integrals, screened_blocks, coeff, support, metric, block_order):
    vm = pltpu.VMEM
    dma = pltpu.SemaphoreType.DMA
    any_spec = pl.BlockSpec(memory_space=pl.ANY)
    res = pl.pallas_call(
        kernel,
        out_shape=jax.ShapeDtypeStruct((SH, NZ * ORB), F32),
        in_specs=[any_spec] * 6,
        out_specs=pl.BlockSpec(memory_space=pltpu.VMEM),
        scratch_shapes=[
            vm((ORB, NSUP, SH), BF16),
            vm((3, NT), I32),
            vm((NZ, NSUP), I32),
            vm((1, 32), I32),
            vm((24, 128), I32),
            vm((24, 128), I32),
            pltpu.SMEM((2, 24, 128), I32),
            vm((NT, AB, SH, SH), BF16),
            vm((NZ // 2, NSUP + 1, ORB, SH), BF16),
            vm((NZ // 2, NSUP + 1, ORB, SH), BF16),
            vm((NSUP + 1, ORB, SH), BF16),
            vm((NSUP * ORB, SH), F32),
            vm((PER_LOAD, 128, SH), F32),
            vm((NT, 128, SH), BF16),
            vm((NT, 64, SH), BF16),
            vm((NC, NT, 64, SH), BF16),
            vm((NC, NT + 1, 32, SH), F32),
            vm((NC, 4, 4, 128, 128), BF16),
            vm((NC, 4, 4, 128, 128), BF16),
            vm((NC, 4, 4, 128, 128), BF16),
            vm((NC, 4, 4, 128, 128), BF16),
            vm((4, 4, 256, SH), BF16),
            vm((4, 4, 256, SH), BF16),
            vm((2, 2, 4, 2, 256, SH), F32),
            vm((2, 2, 3, 2, 256, SH), BF16),
            vm((NC, 3, 2, 2, 2, 128, SH), BF16),
            vm((2, 2, 2, 128, SH), BF16),
            vm((2, 2, 2, 128, SH), BF16),
            vm((2, 4, 128, SH), F32),
            vm((128 * ORB, SH), F32),
            vm((NT, AB * SH, SH), BF16),
            vm((NT, ORB, SH), F32),
            vm((NC, 16, ORB, SH), F32),
            vm((16, ORB, SH), F32),
            vm((16, ORB, SH), F32),
            vm((16, ORB, SH), F32),
            vm((NZ, ORB, SH), F32),
            dma((6,)), dma((LOADS,)), dma((2,)),
            dma((7,)), dma((7,)), dma((3, 3)), dma((3, 3)), dma((4, 3)), dma((4, 3)),
            dma((2, 3)), dma((2, 3)), dma((2,)), dma((2,)),
            dma((5,)), dma((5,)),
            dma((2, 3, 2, 2)), dma((2, 3, 2, 2)), dma((2, 2, 3, 2)), dma((2, 2, 3, 2)), dma((2, 2)), dma((2, 2)),
            dma((15,)), dma((15,)), dma((7,)), dma((7,)),
        ],
        compiler_params=pltpu.CompilerParams(
            collective_id=0, has_side_effects=True, vmem_limit_bytes=56 * 1024 * 1024
        ),
        cost_estimate=pl.CostEstimate(flops=4 * 10**9, bytes_accessed=10 * 10**6, transcendentals=0),
        name="exchange",
    )(integrals, coeff, metric, screened_blocks.T, support, block_order.reshape(1, -1))
    return res.T[None]


def solution(mesh):
    in_specs = (
        P("aux", None, None, None),
        P("aux", None),
        P("occ", None, None),
        P(),
        P("aux", None),
        P(),
    )
    return jax.shard_map(
        body, mesh=mesh, in_specs=in_specs, out_specs=P("aux", None, None), check_vma=False
    )
```

time: 66.9 us -> 63.6 us (0.951)
  Pallas kernels: 63.9 us -> 61.9 us
  local copies, waits for them, and re-layouts: 2.84 us -> 1.57 us
    unnamed x2 -> x0, local copies, waits for them, and re-layouts: 2.84 us -> none
    pallas_call x1, Pallas kernels: 63.9 us -> 61.9 us  [body(): pl.pallas_call(kernel, out_shape=jax.ShapeDtypeStruct((SH, NZ * ORB), F32...]
    broadcast_in_dim x0 -> x1, local copies, waits for them, and re-layouts: none -> 1.57 us  [body(): return res.T[None]]
where the time goes in v3:
time: 63.6 us; the launch traced here: 63.4 us
  Pallas kernels  61.9 us (97%)
  local copies, waits for them, and re-layouts  1.57 us (2%)
    pallas_call x1, Pallas kernels, body(): pl.pallas_call(kernel, out_shape=jax.ShapeDtypeStruct((SH, NZ * ORB), F32...  61.9 us
    broadcast_in_dim x1, local copies, waits for them, and re-layouts, body(): return res.T[None]  1.57 us

profile of v3, /device:TPU:2, one launch (start us, length us, event | category | flops | bytes accessed | tf_op | source)
XLA Modules:
  0.0 63.4 jit_solution(6889157121152921508)
XLA Ops:
  0.0 61.9 %exchange.1 = f32[128,128]{1,0:T(8,128)} custom-call(bf16[32,8,128,128]{3,2,1,0:T(8,128)(2,1)} %ints.1, bf16[16,24,128]{2,1,0:T(8,128)(2,1)} %coeff.1, bf16[128,4096]{1,0:T(8,128)(2,1)} %metric.1, s32[3,32]{1,0:T(4,128)} %bitcast.6, s32[8,24]{1,0:T(8,128)} %support.1, s32[1,32]{1,0:T(1,128)} %bitcast.7), custom_call_target="tpu_custom_call" | custom-call | flops 4000000000 | bytes 10000000 | tf_op jit(solution)/shard_map/exchange/pallas_call | solution.py:486
  61.9 1.6 %copy.7 = f32[1,128,128]{2,1,0:T(8,128)} copy(f32[1,128,128]{1,2,0:T(8,128)} %bitcast.5) | data formatting | bytes 131072 | tf_op jit(solution)/shard_map/broadcast_in_dim | solution.py:542

commit v4 on v3

--- a/solution.py
+++ b/solution.py
@@ -176,7 +176,7 @@
 
     for k in (7, 1, 6, 4, 3, 5, 2):
         start(copy(cown.at[piece(0)], spot(NZ - k).at[piece(0)], zc_s.at[k - 1], zc_r.at[k - 1], zpeer(k)))
-    for k in (2, 1, 3):
+    def metric_send(k):
         for h, (buf, me, to) in enumerate(quarters):
             for m in range(4):
                 part = buf.at[c, me[0], m]
@@ -184,6 +184,8 @@
             part = buf.at[c, me[0]]
             pending.append(copy(part, part, ms_s.at[h, k - 1], ms_r.at[h, k - 1], to(k)))
 
+    metric_send(1)
+    metric_send(3)
     fill_tables(sbv, suv, bov, tabv)
     own_tab = pltpu.make_async_copy(tabv, stab.at[0], tab_sem.at[0])
     own_tab.start()
@@ -231,6 +233,7 @@
     zwait(1)
     zwait(2)
     spread(0)
+    metric_send(2)
     half_loads(LOADS // 2, LOADS)
 
     rows_c = pl.ds(pl.multiple_of(c * 64, 64), 64)
@@ -254,14 +257,6 @@
         for k in (0, 1, 3, 2):
             part = batch(b, piece_n(k))
             copy(part, part, cc_s.at[k, b], cc_r.at[k, b], sibling).wait_recv()
-
-    mfs = []
-    for h, (buf, me, to) in enumerate(quarters):
-        pltpu.make_async_copy(buf.at[c, me[0]], buf.at[c, me[0]], in_sem.at[4 + h]).wait()
-        for k in (1, 3, 2):
-            part = buf.at[c, me[4 - k]]
-            copy(part, part, ms_s.at[h, k - 1], ms_r.at[h, k - 1], sibling).wait_recv()
-        mfs.append(start(copy(buf.at[c], buf.at[c], mf_s.at[h], mf_r.at[h], sibling)))
 
     def transpose_quarters(cc):
         @pl.loop(0, 4)
@@ -277,7 +272,6 @@
     for b in (1, 0):
         for k in (1, 3, 2):
             relay(k, b)
-    transpose_quarters(c)
     for b in (1, 0):
         got_panel(b)
 
@@ -304,10 +298,10 @@
         part = m_part(h, me[0], j, s)
         return copy(part, part, mg_s.at[h, k - 1, j, s], mg_r.at[h, k - 1, j, s], to(k))
 
-    def m_wait(h, j):
+    def m_wait(h, j, ks):
         me, to = ring(h)
         for s in range(NC):
-            for k in (1, 3, 2):
+            for k in ks:
                 part = m_part(h, me[4 - k], j, s)
                 copy(part, part, mg_s.at[h, k - 1, j, s], mg_r.at[h, k - 1, j, s], sibling).wait_recv()
 
@@ -322,10 +316,8 @@
         @pl.loop(0, NT, unroll=8)
         def _(k):
             part = panel(stab[s, NUS, k], (g,))
-            none = jnp.zeros_like(part)
-            rhs = [jnp.concatenate([part, none], axis=1), jnp.concatenate([none, part], axis=1)]
-            lhs = jnp.concatenate([bps[s, k, :32], bps[s, k, 32:]], axis=1)
-            term = lax.dot_general(lhs, jnp.concatenate(rhs, axis=0), nt, preferred_element_type=F32)
+            term = lax.dot_general(bps[s, k], part, nt, preferred_element_type=F32)
+            term = jnp.concatenate([term[:32], term[32:]], axis=1)
             rbuf[s, k + 1] = term + pick(stab[s, KEEP, k], rbuf[s, k])
 
         for h in range(NQ // 2):
@@ -354,28 +346,22 @@
             for a in range(AB):
                 bfull[t, pl.ds(a * SH, SH), :] = blk[:, a * SH : (a + 1) * SH]
 
-    def fit(h, j):
-        got = (mg0, mg1)[h]
-        rhs = [jnp.concatenate([got[m, 2 * j], got[m, 2 * j + 1]], axis=1) for m in range(4)]
-        rhs = jnp.concatenate(rhs, axis=0)
+    def fit(h, j, near):
+        got, me = (mg0, mg1)[h], (ys, xs)[h]
+        blocks = [me[k] for k in ((0, 1, 3) if near else (2,))]
+        rhs = [jnp.concatenate([got[m, 2 * j], got[m, 2 * j + 1]], axis=1) for m in blocks]
         same, cross = ((natt, tra), (nat, trat))[h]
-        if h == 0:
-            lhs = [
-                [(same if cr == ck else cross)[cr, r, k] for k in range(4) for ck in range(NC)]
-                for r in range(4)
-                for cr in range(NC)
-            ]
-        else:
-            lhs = [
-                [(same if cr == ck else cross)[ck, r, k] for k in range(4) for ck in range(NC)]
-                for r in range(4)
-                for cr in range(NC)
-            ]
+        lhs = [
+            [(same if cr == ck else cross)[(cr, ck)[h], r, m] for m in blocks for ck in range(NC)]
+            for r in range(4)
+            for cr in range(NC)
+        ]
         lhs = jnp.concatenate([jnp.concatenate(v, axis=1) for v in lhs], axis=0)
-        res = jnp.dot(lhs, rhs, preferred_element_type=F32)
+        res = jnp.dot(lhs, jnp.concatenate(rhs, axis=0), preferred_element_type=F32)
         for r in range(4):
-            fo[h, j, r, 0] = res[r * 256 : (r + 1) * 256, :SH]
-            fo[h, j, r, 1] = res[r * 256 : (r + 1) * 256, SH:]
+            for u in range(2):
+                part = res[r * 256 : (r + 1) * 256, u * SH : (u + 1) * SH]
+                fo[h, j, r, u] = part if near else fo[h, j, r, u] + part
 
     def f_part(h, j, off):
         return fo.at[h, j, (xs, ys)[h][off]]
@@ -393,8 +379,11 @@
 
     def fits(j):
         for h in range(2):
-            m_wait(h, j)
-            fit(h, j)
+            m_wait(h, j, (1, 3))
+            fit(h, j, True)
+        for h in range(2):
+            m_wait(h, j, (2,))
+            fit(h, j, False)
             for k in (2, 1, 3):
                 fsend[h, j, k - 1] = f_part(h, j, k)[...].astype(BF16)
                 for cc in range(NC):
@@ -429,10 +418,20 @@
 
     m_terms(1, 0)
     m_terms(1, 1)
+    mfs = []
+    for h, (buf, me, to) in enumerate(quarters):
+        pltpu.make_async_copy(buf.at[c, me[0]], buf.at[c, me[0]], in_sem.at[4 + h]).wait()
+        for k in (1, 3, 2):
+            part = buf.at[c, me[4 - k]]
+            copy(part, part, ms_s.at[h, k - 1], ms_r.at[h, k - 1], sibling).wait_recv()
+        mfs.append(start(copy(buf.at[c], buf.at[c], mf_s.at[h], mf_r.at[h], sibling)))
+
+    full_blocks(0, 4)
+    transpose_quarters(c)
     for cp in mfs:
         cp.wait_recv()
     transpose_quarters(1 - c)
-    full_blocks(0, 10)
+    full_blocks(4, 10)
     fits(0)
     full_blocks(10, 24)
     fits(1)
@@ -473,7 +472,10 @@
     for k in (1, 7, 2, 6, 3, 5, 4):
         got = zall.at[zs[NZ - k]]
         copy(got, got, z_s.at[k - 1], z_r.at[k - 1], zpeer(k)).wait_recv()
-    out[...] = zall[...].reshape(NZ * ORB, SH)
+    whole = zall[...].reshape(NZ * ORB, SH).T
+    even = lax.rem(lax.broadcasted_iota(I32, whole.shape, 0), 2) == 0
+    out[0] = jnp.where(even, whole, 0.0)
+    out[1] = jnp.where(even, 0.0, whole)
 
     for cp in pending:
         cp.wait_send()
@@ -485,7 +487,7 @@
     any_spec = pl.BlockSpec(memory_space=pl.ANY)
     res = pl.pallas_call(
         kernel,
-        out_shape=jax.ShapeDtypeStruct((SH, NZ * ORB), F32),
+        out_shape=jax.ShapeDtypeStruct((2, SH, NZ * ORB), F32),
         in_specs=[any_spec] * 6,
         out_specs=pl.BlockSpec(memory_space=pltpu.VMEM),
         scratch_shapes=[
@@ -539,7 +541,7 @@
         cost_estimate=pl.CostEstimate(flops=4 * 10**9, bytes_accessed=10 * 10**6, transcendentals=0),
         name="exchange",
     )(integrals, coeff, metric, screened_blocks.T, support, block_order.reshape(1, -1))
-    return res.T[None]
+    return (res[0] + res[1])[None]
 
 
 def solution(mesh):

time: 63.6 us -> 61 us (0.959)
  Pallas kernels: 61.9 us -> 59.3 us
  local copies, waits for them, and re-layouts: 1.57 us -> 0 us
  other arithmetic: 0 us -> 1.51 us
    pallas_call x1, Pallas kernels: 61.9 us -> 59.3 us  [body(): pl.pallas_call(kernel, out_shape=jax.ShapeDtypeStruct((2, SH, NZ * ORB),...]
    broadcast_in_dim x1 -> x0, local copies, waits for them, and re-layouts: 1.57 us -> none  [body(): return res.T[None]]
    add x0 -> x1, other arithmetic: none -> 1.51 us  [body(): return (res[0] + res[1])[None]]
where the time goes in v4:
time: 61 us; the launch traced here: 60.8 us
  Pallas kernels  59.3 us (97%)
  other arithmetic  1.51 us (2%)
    pallas_call x1, Pallas kernels, body(): pl.pallas_call(kernel, out_shape=jax.ShapeDtypeStruct((2, SH, NZ * ORB),...  59.3 us
    add x1, other arithmetic, body(): return (res[0] + res[1])[None]  1.51 us

profile of v4, /device:TPU:2, one launch (start us, length us, event | category | flops | bytes accessed | tf_op | source)
XLA Modules:
  0.0 60.8 jit_solution(15576914453599903773)
XLA Ops:
  0.0 59.3 %exchange.1 = f32[2,128,128]{2,1,0:T(8,128)} custom-call(bf16[32,8,128,128]{3,2,1,0:T(8,128)(2,1)} %ints.1, bf16[16,24,128]{2,1,0:T(8,128)(2,1)} %coeff.1, bf16[128,4096]{1,0:T(8,128)(2,1)} %metric.1, s32[3,32]{1,0:T(4,128)} %bitcast.2, s32[8,24]{1,0:T(8,128)} %support.1, s32[1,32]{1,0:T(1,128)} %bitcast.3), custom_call_target="tpu_custom_call" | custom-call | flops 4000000000 | bytes 10000000 | tf_op jit(solution)/shard_map/exchange/pallas_call | solution.py:488
  59.3 1.5 %slice_add_fusion = f32[1,128,128]{2,1,0:T(8,128)} fusion(f32[2,128,128]{2,1,0:T(8,128)} %exchange.1), kind=kLoop, calls=%fused_computation | loop fusion | flops 16384 | bytes 196608 | tf_op jit(solution)/shard_map/add | solution.py:544

commit v5 on v4

--- a/solution.py
+++ b/solution.py
@@ -104,6 +104,10 @@
         pending.append(cp)
         return cp
 
+    def drain(lo, hi):
+        for cp in pending[lo:hi]:
+            cp.wait_send()
+
     def load(i):
         part = pl.ds(i * PER_LOAD, PER_LOAD)
         return pltpu.make_async_copy(ints.at[part], iv.at[part], int_sem.at[i])
@@ -432,9 +436,11 @@
         cp.wait_recv()
     transpose_quarters(1 - c)
     full_blocks(4, 10)
+    marks = [len(pending)]
     fits(0)
     full_blocks(10, 24)
     fits(1)
+    drain(0, marks[0])
     full_blocks(24, NT)
     totals(0)
     totals(1)
@@ -443,7 +449,7 @@
     low = pl.ds(pl.multiple_of(c * JL, JL), JL)
     high = pl.ds(pl.multiple_of((1 - c) * JL, JL), JL)
 
-    @pl.loop(0, NT, unroll=8)
+    @pl.loop(0, NT, unroll=16)
     def _(t):
         rows = ftq[stab[0, QQ, t]]
         lhs = jnp.concatenate([rows[a * ORB : (a + 1) * ORB] for a in range(AB)], axis=1)
@@ -459,16 +465,20 @@
     g_send = start(copy(gs.at[1 - c], gr, ex_s.at[4], ex_r.at[4], sibling))
     g_send.wait_recv()
     gx[...] = gs[c] + gr[...]
+    marks.append(len(pending))
     for k in (10, 6, 14, 9, 11, 5, 7, 13, 15, 2, 8, 1, 3, 4, 12):
         yy, xx = plane(k)
         start(copy(gx.at[yy * NX + xx], gin.at[k], gx_s.at[k - 1], gx_r.at[k - 1], dev(yy, xx, c, z)))
+    drain(marks[0], marks[1])
     total = gx[y * NX + x]
     for k in (1, 3, 4, 12, 2, 8, 5, 7, 13, 15, 6, 14, 9, 11, 10):
         copy(gx.at[0], gin.at[k], gx_s.at[k - 1], gx_r.at[k - 1], sibling).wait_recv()
         total = total + gin[k]
+    marks.append(len(pending))
     zall[z] = total
     for k in (4, 3, 5, 2, 6, 1, 7):
         start(copy(zall.at[z], zall.at[z], z_s.at[k - 1], z_r.at[k - 1], zpeer(k)))
+    drain(marks[1], marks[2])
     for k in (1, 7, 2, 6, 3, 5, 4):
         got = zall.at[zs[NZ - k]]
         copy(got, got, z_s.at[k - 1], z_r.at[k - 1], zpeer(k)).wait_recv()
@@ -477,8 +487,7 @@
     out[0] = jnp.where(even, whole, 0.0)
     out[1] = jnp.where(even, 0.0, whole)
 
-    for cp in pending:
-        cp.wait_send()
+    drain(marks[2], len(pending))
 
 
 def body(integrals, screened_blocks, coeff, support, metric, block_order):

time: 61 us -> 60.6 us (level)
  no operation moved by 1% of the time
where the time goes in v5:
time: 60.6 us; the launch traced here: 60.4 us
  Pallas kernels  58.9 us (97%)
  other arithmetic  1.51 us (2%)
    pallas_call x1, Pallas kernels, body(): pl.pallas_call(kernel, out_shape=jax.ShapeDtypeStruct((2, SH, NZ * ORB),...  58.9 us
    add x1, other arithmetic, body(): return (res[0] + res[1])[None]  1.51 us

profile of v5, /device:TPU:2, one launch (start us, length us, event | category | flops | bytes accessed | tf_op | source)
XLA Modules:
  0.0 60.4 jit_solution(3481542726116911202)
XLA Ops:
  0.0 58.9 %exchange.1 = f32[2,128,128]{2,1,0:T(8,128)} custom-call(bf16[32,8,128,128]{3,2,1,0:T(8,128)(2,1)} %ints.1, bf16[16,24,128]{2,1,0:T(8,128)(2,1)} %coeff.1, bf16[128,4096]{1,0:T(8,128)(2,1)} %metric.1, s32[3,32]{1,0:T(4,128)} %bitcast.2, s32[8,24]{1,0:T(8,128)} %support.1, s32[1,32]{1,0:T(1,128)} %bitcast.3), custom_call_target="tpu_custom_call" | custom-call | flops 4000000000 | bytes 10000000 | tf_op jit(solution)/shard_map/exchange/pallas_call | solution.py:497
  58.9 1.5 %slice_add_fusion = f32[1,128,128]{2,1,0:T(8,128)} fusion(f32[2,128,128]{2,1,0:T(8,128)} %exchange.1), kind=kLoop, calls=%fused_computation | loop fusion | flops 16384 | bytes 196608 | tf_op jit(solution)/shard_map/add | solution.py:553

commit v6 on v5

--- a/solution.py
+++ b/solution.py
@@ -317,7 +317,7 @@
     def m_terms(g, s):
         rbuf[s, 0] = jnp.zeros((32, SH), F32)
 
-        @pl.loop(0, NT, unroll=8)
+        @pl.loop(0, NT, unroll=16)
         def _(k):
             part = panel(stab[s, NUS, k], (g,))
             term = lax.dot_general(bps[s, k], part, nt, preferred_element_type=F32)
@@ -482,10 +482,7 @@
     for k in (1, 7, 2, 6, 3, 5, 4):
         got = zall.at[zs[NZ - k]]
         copy(got, got, z_s.at[k - 1], z_r.at[k - 1], zpeer(k)).wait_recv()
-    whole = zall[...].reshape(NZ * ORB, SH).T
-    even = lax.rem(lax.broadcasted_iota(I32, whole.shape, 0), 2) == 0
-    out[0] = jnp.where(even, whole, 0.0)
-    out[1] = jnp.where(even, 0.0, whole)
+    out[...] = zall[...].reshape(NZ * ORB, SH).T
 
     drain(marks[2], len(pending))
 
@@ -496,7 +493,7 @@
     any_spec = pl.BlockSpec(memory_space=pl.ANY)
     res = pl.pallas_call(
         kernel,
-        out_shape=jax.ShapeDtypeStruct((2, SH, NZ * ORB), F32),
+        out_shape=jax.ShapeDtypeStruct((SH, NZ * ORB), F32),
         in_specs=[any_spec] * 6,
         out_specs=pl.BlockSpec(memory_space=pltpu.VMEM),
         scratch_shapes=[
@@ -550,7 +547,7 @@
         cost_estimate=pl.CostEstimate(flops=4 * 10**9, bytes_accessed=10 * 10**6, transcendentals=0),
         name="exchange",
     )(integrals, coeff, metric, screened_blocks.T, support, block_order.reshape(1, -1))
-    return (res[0] + res[1])[None]
+    return res[None]
 
 
 def solution(mesh):

time: 60.6 us -> 59.8 us (0.987)
  other arithmetic: 1.51 us -> 0 us
  local copies, waits for them, and re-layouts: 0 us -> 1.47 us
  Pallas kernels: 58.9 us -> 58 us
    add x1 -> x0, other arithmetic: 1.51 us -> none  [body(): return (res[0] + res[1])[None]]
    unnamed x0 -> x1, local copies, waits for them, and re-layouts: none -> 1.47 us
    pallas_call x1, Pallas kernels: 58.9 us -> 58 us  [body(): pl.pallas_call(kernel, out_shape=jax.ShapeDtypeStruct((SH, NZ * ORB), F32...]
where the time goes in v6:
time: 59.8 us; the launch traced here: 59.5 us
  Pallas kernels  58 us (97%)
  local copies, waits for them, and re-layouts  1.47 us (2%)
    pallas_call x1, Pallas kernels, body(): pl.pallas_call(kernel, out_shape=jax.ShapeDtypeStruct((SH, NZ * ORB), F32...  58 us
    unnamed x1, local copies, waits for them, and re-layouts  1.47 us

profile of v6, /device:TPU:2, one launch (start us, length us, event | category | flops | bytes accessed | tf_op | source)
XLA Modules:
  0.0 59.5 jit_solution(9593882101691874411)
XLA Ops:
  0.0 58.0 %exchange.1 = f32[128,128]{1,0:T(8,128)} custom-call(bf16[32,8,128,128]{3,2,1,0:T(8,128)(2,1)} %ints.1, bf16[16,24,128]{2,1,0:T(8,128)(2,1)} %coeff.1, bf16[128,4096]{1,0:T(8,128)(2,1)} %metric.1, s32[3,32]{1,0:T(4,128)} %bitcast.4, s32[8,24]{1,0:T(8,128)} %support.1, s32[1,32]{1,0:T(1,128)} %bitcast.5), custom_call_target="tpu_custom_call" | custom-call | flops 4000000000 | bytes 10000000 | tf_op jit(solution)/shard_map/exchange/pallas_call | solution.py:494
  58.0 1.5 %copy.8 = f32[1,128,128]{2,1,0:T(8,128)} copy(f32[1,128,128]{2,1,0:T(8,128)} %bitcast.3) | data formatting | bytes 131072
